TPU v7x, 512 devices: a whole 4x8x8 slice. The times are simulated.
512 devices in a mesh: row: 32 (over z, x), col: 16 (over y, core).
Axes of the slice: x: 4, y: 8, z: 8, core: 2. Of those that a mesh axis runs over, the one named last changes fastest.
Arguments:
- hamiltonian: float32 [24576, 24576], P('row', 'col'), may hold values from -1 to 4, as said below
- search_block: float32 [24576, 256], P(('col', 'row')), may hold values from -6 to 6
- filter_bounds: float32 [3], replicated, may hold values from -2 to 6, as said below
Outputs:
- first_filtered: float32 [24576, 256], P(('row', 'col'))
- second_filtered: float32 [24576, 256], P(('col', 'row'))
Inputs may be any that keep to these rules, and one draw needn't show every extreme that they name: `hamiltonian`: symmetric; its diagonal dominates each entry off it. `filter_bounds`: increasing: lower < low_end < high_end, lower below the spectrum and high_end above it.
All inputs are finite; a program needn't handle non-finite values.
Results may differ from a plain program's by a relative error of at most 0.000092.
Values sent between devices are 32-bit elements; how exact they have to be, the bound alone decides.
No kernel may reach another device: no remote copies, remote signals or barrier semaphores. Data moves between devices by JAX's collectives and lax.ppermute only.
A program may use at most 64 MiB of HBM per device.

v0:
```python
import jax
import jax.numpy as jnp
from jax import lax
from jax.sharding import PartitionSpec as P


def body(hamiltonian, search_block, filter_bounds):
    lower = filter_bounds[0]
    low_end = filter_bounds[1]
    high_end = filter_bounds[2]
    center = (high_end + low_end) / 2.0
    half = (high_end - low_end) / 2.0
    sigma_one = half / (lower - center)
    sigma_two = 1.0 / (2.0 / sigma_one - sigma_one)
    scale_one = sigma_one / half
    scale_two = 2.0 * sigma_two / half
    damp = sigma_two * sigma_one
    rows_tile, cols_tile = hamiltonian.shape
    col_count = lax.axis_size("col")
    row_place = lax.axis_index("row")
    col_place = lax.axis_index("col")
    global_rows = row_place * rows_tile + jnp.arange(rows_tile, dtype=jnp.int32)[:, None]
    global_cols = col_place * cols_tile + jnp.arange(cols_tile, dtype=jnp.int32)[None, :]
    shifted = hamiltonian - center * (global_rows == global_cols).astype(jnp.float32)
    column_block = lax.all_gather(search_block, "row", axis=0, tiled=True)
    share = rows_tile // col_count
    partial_rows = jnp.dot(
        shifted, column_block, preferred_element_type=jnp.float32, precision=lax.Precision.HIGHEST
    )
    first_rows = scale_one * lax.psum(partial_rows, "col")
    first_out = lax.dynamic_slice_in_dim(first_rows, col_place * share, share, 0)
    summed_two = lax.psum_scatter(
        lax.dot_general(
            shifted,
            first_rows,
            (((0,), (0,)), ((), ())),
            precision=lax.Precision.HIGHEST,
            preferred_element_type=jnp.float32,
        ),
        "row",
        scatter_dimension=0,
        tiled=True,
    )
    second_out = scale_two * summed_two - damp * search_block
    return (first_out, second_out)


def solution(mesh):
    placed = (P("row", "col"), P(("col", "row"), None), P())
    return jax.shard_map(
        body,
        mesh=mesh,
        in_specs=placed,
        out_specs=(P(("row", "col"), None), P(("col", "row"), None)),
        check_vma=False,
    )
```

profile of v0, /device:TPU:1, one launch (start us, length us, event | category | flops | bytes accessed | tf_op | source)
XLA Modules:
  0.0 459.2 jit_solution(14500077185546648470)
XLA Ops:
  7.2 0.0 all-gather.2.cloned.1.call-start
  7.2 0.7 all-gather.2.cloned.1.call-update
  7.9 0.0 all-reduce.2.cloned.1.call-start
  7.9 1.4 fusion.12
  10.6 85.6 %all-gather.2.cloned.1.call-done = f32[1536,256]{1,0:T(8,128)} async-done(((f32[48,256]{1,0:T(8,128)}), f32[1536,256]{1,0:T(8,128)}) %all-gather.2.cloned.1.call-update) | async-done | bytes 1572880 | tf_op jit(solution)/shard_map/all_gather | solution.py:25
  96.2 7.8 %fusion.1 = f32[768,256]{1,0:T(8,128)} fusion(f32[1536,256]{1,0:T(8,128)} %all-gather.2.cloned.1.call-done, f32[768,1536]{1,0:T(8,128)} %param.3, f32[]{:T(128)} %bitcast.2, s32[1536]{0:T(1024)S(1)} %iota_add_fusion, s32[768]{0:T(1024)S(1)} %iota_add_fusion.1), kind=kOutput, calls=%fused_computation.2 | convolution fusion | flops 3627417600 | bytes 7087108 | tf_op jit(solution)/shard_map/dot_general | solution.py:27
  104.0 0.0 all-reduce.2.cloned.1.call-update
  104.0 0.2 reduce-scatter.2.cloned.1.call-start
  106.2 114.5 %all-reduce.2.cloned.1.call-done = f32[768,256]{1,0:T(8,128)} async-done(((f32[768,256]{1,0:T(8,128)}), f32[768,256]{1,0:T(8,128)}) %all-reduce.2.cloned.1.call-update) | async-done | bytes 786448 | tf_op jit(solution)/shard_map/psum | solution.py:30
  220.8 1.2 broadcast_multiply_fusion
  221.9 0.0 copy-start
  222.0 11.2 %fusion = f32[1536,256]{1,0:T(8,128)} fusion(f32[768,256]{1,0:T(8,128)S(1)} %broadcast_multiply_fusion, f32[768,1536]{1,0:T(8,128)} %param.3, f32[]{:T(128)} %bitcast.2, s32[1536]{0:T(1024)S(1)} %iota_add_fusion, s32[768]{0:T(1024)S(1)} %iota_add_fusion.1), kind=kOutput, calls=%fused_computation.1 | convolution fusion | flops 3627417600 | bytes 7087108 | tf_op jit(solution)/shard_map/dot_general | solution.py:33
  233.1 0.0 reduce-scatter.2.cloned.1.call-update
  233.3 0.6 constant_dynamic-slice_fusion
  234.0 217.3 %reduce-scatter.2.cloned.1.call-done = f32[48,256]{1,0:T(8,128)} async-done(((f32[1536,256]{1,0:T(8,128)}), f32[48,256]{1,0:T(8,128)}) %reduce-scatter.2.cloned.1.call-update) | async-done | bytes 49168 | tf_op jit(solution)/shard_map/reduce_scatter | solution.py:32
  451.3 0.0 copy-done
  451.3 1.4 multiply_subtract_fusion
  (2 shorter events, 0.0 us)
Async XLA Ops:
  7.2 89.0 %all-gather.2.cloned.1.call-start = ((), (), s32[]{:S(2)}) async-start(), calls=%async_computation.1 | async-start | bytes 1622016 | tf_op jit(solution)/shard_map/all_gather | solution.py:25
  7.9 212.9 %all-reduce.2.cloned.1.call-start = ((), (), s32[]{:S(2)}) async-start(), calls=%async_computation.2 | async-start | bytes 1572864 | tf_op jit(solution)/shard_map/psum | solution.py:30
  104.0 347.2 %reduce-scatter.2.cloned.1.call-start = ((), (), s32[]{:S(2)}) async-start(), calls=%async_computation.3 | async-start | bytes 1622016 | tf_op jit(solution)/shard_map/reduce_scatter | solution.py:32
  221.9 229.3 %copy-start = (f32[48,256]{1,0:T(8,128)S(1)}, f32[48,256]{1,0:T(8,128)}, u32[]{:S(2)}) copy-start(f32[48,256]{1,0:T(8,128)} %param.4) | copy-start | bytes 147460
Sparse Core Ops, SparseCore 0:
  11.2 85.0 all-gather.1
  104.2 116.5 all-reduce.1
  233.3 217.9 reduce-scatter.1
where the time goes:
time: 464 us; the launch traced here: 459 us
  waiting for transfers between devices  418 us (90%)
  matrix products  19 us (4%)
  between operations  17.2 us (4%)
    reduce_scatter x1, waiting for transfers between devices, body(): lax.psum_scatter(lax.dot_general(shifted, first_rows, (((0,), (0,)), ((),...  217 us
    psum x1, waiting for transfers between devices, body(): first_rows = scale_one * lax.psum(partial_rows, 'col')  115 us
    all_gather x1, waiting for transfers between devices, body(): column_block = lax.all_gather(search_block, 'row', axis=0, tiled=True)  85.6 us
    dot_general x1, matrix products, body(): lax.dot_general(shifted, first_rows, (((0,), (0,)), ((), ())), precision=...  11.2 us
  transfers between devices with their start and end apart: 3, of which 3 were waited for; matrix products, arithmetic and copies ran while one was open for 0% of the time, Pallas kernels for 0%

commit v1 on v0

v1 whole, which is shorter than its diff:
```python
import jax
import jax.numpy as jnp
from jax import lax
from jax.sharding import Mesh, PartitionSpec as P


def body(hamiltonian, search_block, filter_bounds):
    lower = filter_bounds[0]
    low_end = filter_bounds[1]
    high_end = filter_bounds[2]
    center = (high_end + low_end) / 2.0
    half = (high_end - low_end) / 2.0
    sigma_one = half / (lower - center)
    sigma_two = 1.0 / (2.0 / sigma_one - sigma_one)
    scale_one = sigma_one / half
    scale_two = 2.0 * sigma_two / half
    damp = sigma_two * sigma_one

    zs, xs, ys, cs = (lax.axis_size(a) for a in ("z", "x", "y", "c"))
    z, x, y, c = (lax.axis_index(a) for a in ("z", "x", "y", "c"))
    rows_tile, cols_tile = hamiltonian.shape
    piece, width = search_block.shape
    part = width // cs
    swap = [(i, cs - 1 - i) for i in range(cs)]

    other = lax.ppermute(hamiltonian, "c", swap)
    global_rows = (z * xs + x) * rows_tile + jnp.arange(rows_tile, dtype=jnp.int32)[:, None]

    def shift(tile, core):
        global_cols = (y * cs + core) * cols_tile + jnp.arange(cols_tile, dtype=jnp.int32)[None, :]
        return tile - center * (global_rows == global_cols).astype(jnp.float32)

    mine = shift(hamiltonian, c)
    theirs = shift(other, cs - 1 - c)

    halves = search_block.reshape(piece, cs, part).transpose(1, 0, 2)
    sent = jnp.broadcast_to(halves[None], (zs, cs, piece, part)).reshape(zs * cs, piece, part)
    got = lax.all_to_all(sent, ("z", "c"), 0, 0, tiled=True)
    sent = jnp.broadcast_to(got[None], (xs,) + got.shape)
    got = lax.all_to_all(sent, "x", 0, 0, tiled=True)
    got = got.reshape(xs, zs, cs, piece, part).transpose(2, 1, 0, 3, 4).reshape(cs, cols_tile, part)
    got_mine = lax.dynamic_index_in_dim(got, c, 0, keepdims=False)
    got_theirs = lax.dynamic_index_in_dim(got, cs - 1 - c, 0, keepdims=False)

    def dot(a, b, dims):
        return lax.dot_general(
            a, b, (dims, ((), ())), precision=lax.Precision.HIGH, preferred_element_type=jnp.float32
        )

    partial_rows = dot(mine, got_mine, ((1,), (0,))) + dot(theirs, got_theirs, ((1,), (0,)))
    share = rows_tile // ys
    terms = lax.all_to_all(partial_rows.reshape(ys, share, part), "y", 0, 0, tiled=True)
    first = scale_one * terms.sum(0)
    sent = jnp.broadcast_to(first[None], (ys, share, part))
    first_rows = lax.all_to_all(sent, "y", 0, 0, tiled=True).reshape(rows_tile, part)

    first_pair = first.reshape(cs, piece, part)
    keep = lax.dynamic_index_in_dim(first_pair, c, 0, keepdims=False)
    give = lax.dynamic_index_in_dim(first_pair, cs - 1 - c, 0, keepdims=False)
    came = lax.ppermute(give, "c", swap)
    first_out = jnp.where(c == 0, jnp.concatenate([keep, came], 1), jnp.concatenate([came, keep], 1))

    out_mine = dot(mine, first_rows, ((0,), (0,)))
    out_theirs = dot(theirs, first_rows, ((0,), (0,)))
    both = jnp.where(c == 0, jnp.stack([out_mine, out_theirs]), jnp.stack([out_theirs, out_mine]))
    sent = both.reshape(cs, zs, xs, piece, part).transpose(2, 1, 0, 3, 4).reshape(xs, zs * cs, piece, part)
    summed = lax.all_to_all(sent, "x", 0, 0, tiled=True).sum(0)
    summed = lax.all_to_all(summed, ("z", "c"), 0, 0, tiled=True)
    summed = summed.reshape(zs, cs, piece, part).sum(0).transpose(1, 0, 2).reshape(piece, width)
    second_out = scale_two * summed - damp * search_block
    return (first_out, second_out)


def solution(mesh):
    fine = Mesh(mesh.devices.reshape(8, 4, 8, 2), ("z", "x", "y", "c"))
    row, col = ("z", "x"), ("y", "c")
    return jax.shard_map(
        body,
        mesh=fine,
        in_specs=(P(row, col), P(col + row, None), P()),
        out_specs=(P(row + col, None), P(col + row, None)),
        check_vma=False,
    )
```

time: 464 us -> 166 us (0.36)
  waiting for transfers between devices: 418 us -> 58.1 us
  blocking collectives: 0 us -> 41 us
  starting transfers between devices: 0.3 us -> 31.4 us
  between operations: 17.2 us -> 4.27 us
  local copies, waits for them, and re-layouts: 2 us -> 9.12 us
    reduce_scatter x1 -> x0, waiting for transfers between devices: 217 us -> none  [body(): lax.psum_scatter(lax.dot_general(shifted, first_rows, (((0,), (0,)), ((),...]
    psum x1 -> x0, waiting for transfers between devices: 115 us -> none  [body(): first_rows = scale_one * lax.psum(partial_rows, 'col')]
    all_gather x1 -> x0, waiting for transfers between devices: 85.6 us -> none  [body(): column_block = lax.all_gather(search_block, 'row', axis=0, tiled=True)]
    all_to_all x0 -> x4, waiting for transfers between devices: none -> 57.3 us  [the longest x1 19.3 us: body(): got = lax.all_to_all(sent, 'x', 0, 0, tiled=True)]
    all_to_all x0 -> x2, blocking collectives: none -> 41 us  [the longest x1 21.6 us: body(): summed = lax.all_to_all(sent, 'x', 0, 0, tiled=True).sum(0)]
    all_to_all x0 -> x4, starting transfers between devices: none -> 20.4 us  [the longest x1 6.82 us: body(): lax.all_to_all(partial_rows.reshape(ys, share, part), 'y', 0, 0, tiled=True)]
    ppermute x0 -> x2, starting transfers between devices: none -> 11 us  [the longest x1 8.91 us: body(): other = lax.ppermute(hamiltonian, 'c', swap)]
    unnamed x2 -> x11, local copies, waits for them, and re-layouts: 0.01 us -> 6.09 us
  transfers between devices with their start and end apart: 3 -> 6, of which waited for: 3 -> 5; matrix products, arithmetic and copies ran while one was open for 0% -> 2% of each run, Pallas kernels for 0% -> 0%
where the time goes in v1:
time: 166 us
  waiting for transfers between devices  58.1 us (35%)
  blocking collectives  41 us (25%)
  starting transfers between devices  31.4 us (19%)
  matrix products  15.1 us (9%)
  local copies, waits for them, and re-layouts  9.12 us (5%)
  other arithmetic  6.71 us (4%)
  between operations  4.27 us (3%)
    all_to_all x1, blocking collectives, body(): summed = lax.all_to_all(sent, 'x', 0, 0, tiled=True).sum(0)  21.6 us
    all_to_all x1, blocking collectives, body(): got = lax.all_to_all(sent, ('z', 'c'), 0, 0, tiled=True)  19.4 us
    all_to_all x1, waiting for transfers between devices, body(): got = lax.all_to_all(sent, 'x', 0, 0, tiled=True)  19.3 us
    dot_general x4, matrix products, dot(): lax.dot_general(a, b, (dims, ((), ())), precision=lax.Precision.HIGH, pre...  15.1 us
    all_to_all x1, waiting for transfers between devices, body(): lax.all_to_all(sent, 'y', 0, 0, tiled=True).reshape(rows_tile, part)  14 us
    all_to_all x1, waiting for transfers between devices, body(): lax.all_to_all(partial_rows.reshape(ys, share, part), 'y', 0, 0, tiled=True)  13.2 us
    all_to_all x1, waiting for transfers between devices, body(): summed = lax.all_to_all(summed, ('z', 'c'), 0, 0, tiled=True)  10.8 us
    ppermute x1, starting transfers between devices, body(): other = lax.ppermute(hamiltonian, 'c', swap)  8.91 us
  transfers between devices with their start and end apart: 6, of which 5 were waited for; matrix products, arithmetic and copies ran while one was open for 2% of the time, Pallas kernels for 0%

profile of v1, /device:TPU:1, one launch (start us, length us, event | category | flops | bytes accessed | tf_op | source)
XLA Modules:
  0.0 165.6 jit_solution(17019311312151818140)
XLA Ops:
  0.6 6.1 %copy.22 = f32[768,1536]{0,1:T(8,128)} copy(f32[768,1536]{1,0:T(8,128)} %param.3) | data formatting | bytes 9437184 | tf_op args[0]
  6.7 8.9 %collective-permute-start = (f32[768,1536]{0,1:T(8,128)}, f32[768,1536]{0,1:T(8,128)}, u32[]{:S(2)}, u32[]{:S(2)}) collective-permute-start(f32[768,1536]{0,1:T(8,128)} %copy.22), channel_id=1, source_target_pairs={{0,1},{1,0},{2,3},{3,2},{4,5},{5,4},{6,7},{7,6},{8,9},{9,8},{10,11... | collective-permute-start | bytes 14155784 | tf_op jit(solution)/shard_map/ppermute | solution.py:26
  15.7 19.4 %all_to_all.30 = f32[16,48,128]{2,1,0:T(8,128)S(1)} all-to-all(f32[16,48,128]{2,1,0:T(8,128)S(1)} %bitcast.61), channel_id=1, replica_groups=mesh['z'=8,'x'=4,'y'=8,'c'=2] {'z','c'}, dimensions={0} | all-to-all | bytes 786432 | tf_op jit(solution)/shard_map/all_to_all | solution.py:38
  35.1 1.3 broadcast_in_dim.7
  36.4 4.0 %all-to-all-start.1 = ((f32[4,16,48,128]{3,2,1,0:T(8,128)}), f32[4,16,48,128]{3,2,1,0:T(8,128)S(1)}, u32[]{:S(2)}, u32[]{:S(2)}) async-start(f32[4,16,48,128]{3,2,1,0:T(8,128)} %broadcast_in_dim.7), calls=%async_computation.1 | async-start | bytes 3145728 | tf_op jit(solution)/shard_map/all_to_all | solution.py:40
  42.4 19.3 %all-to-all-done.1 = f32[4,16,48,128]{3,2,1,0:T(8,128)S(1)} async-done(((f32[4,16,48,128]{3,2,1,0:T(8,128)}), f32[4,16,48,128]{3,2,1,0:T(8,128)S(1)}, u32[]{:S(2)}, u32[]{:S(2)}) %all-to-all-start.1) | async-done | bytes 1572896 | tf_op jit(solution)/shard_map/all_to_all | solution.py:40
  61.8 4.4 %select_subtract_fusion = (f32[768,1536]{0,1:T(8,128)S(1)}, f32[768,1536]{0,1:T(8,128)S(1)}) fusion(f32[768,1536]{0,1:T(8,128)} %collective-permute-done, f32[]{:T(128)} %bitcast.2, s32[768]{0:T(1024)S(1)} %iota_add_fusion.2, s32[1536]{0:T(1024)S(1)} %get-tuple-element.9, f32[768,1536]{0,1:T(8,128)} %copy.22, s32[1536]{0:T(1024)S(1)} %get-tuple-element.10), kind=kLoop, calls=%fused_computation | loop fusion | flops 7077888 | bytes 18889732 | tf_op jit(solution)/shard_map/sub | solution.py:31
  66.2 3.9 %fusion.2 = f32[768,128]{1,0:T(8,128)S(1)} fusion(f32[768,1536]{0,1:T(8,128)S(1)} %get-tuple-element.5, f32[2,1536,128]{2,1,0:T(8,128)S(1)} %bitcast.55, s32[]{:T(128)S(6)} %select_n.28), kind=kOutput, calls=%fused_computation.8 | convolution fusion | flops 905969664 | bytes 5898244 | tf_op jit(solution)/shard_map/dot_general | solution.py:46
  70.1 4.7 %convolution_add_fusion = f32[768,128]{1,0:T(8,128)} fusion(f32[768,128]{1,0:T(8,128)S(1)} %fusion.2, f32[768,1536]{0,1:T(8,128)S(1)} %get-tuple-element.4, f32[2,1536,128]{2,1,0:T(8,128)S(1)} %bitcast.56, s32[]{:T(128)S(6)} %select_n.29), kind=kOutput, calls=%fused_computation.6 | convolution fusion | flops 906067968 | bytes 6291460 | tf_op jit(solution)/shard_map/dot_general | solution.py:46
  74.8 6.8 %all-to-all-start.2 = ((f32[8,96,128]{2,1,0:T(8,128)}), f32[8,96,128]{2,1,0:T(8,128)S(1)}, u32[]{:S(2)}, u32[]{:S(2)}) async-start(f32[8,96,128]{2,1,0:T(8,128)} %bitcast.10), calls=%async_computation.2 | async-start | bytes 786432 | tf_op jit(solution)/shard_map/all_to_all | solution.py:52
  83.6 13.2 %all-to-all-done.2 = f32[8,96,128]{2,1,0:T(8,128)S(1)} async-done(((f32[8,96,128]{2,1,0:T(8,128)}), f32[8,96,128]{2,1,0:T(8,128)S(1)}, u32[]{:S(2)}, u32[]{:S(2)}) %all-to-all-start.2) | async-done | bytes 393248 | tf_op jit(solution)/shard_map/all_to_all | solution.py:52
  96.8 0.8 broadcast_in_dim.8
  97.6 3.6 %all-to-all-start.3 = ((f32[8,96,128]{2,1,0:T(8,128)}), f32[8,96,128]{2,1,0:T(8,128)S(1)}, u32[]{:S(2)}, u32[]{:S(2)}) async-start(f32[8,96,128]{2,1,0:T(8,128)} %broadcast_in_dim.8), calls=%async_computation.3 | async-start | bytes 786432 | tf_op jit(solution)/shard_map/all_to_all | solution.py:55
  101.2 14.0 %all-to-all-done.3 = f32[8,96,128]{2,1,0:T(8,128)S(1)} async-done(((f32[8,96,128]{2,1,0:T(8,128)}), f32[8,96,128]{2,1,0:T(8,128)S(1)}, u32[]{:S(2)}, u32[]{:S(2)}) %all-to-all-start.3) | async-done | bytes 393248 | tf_op jit(solution)/shard_map/all_to_all | solution.py:55
  115.2 4.5 %convolution_bitcast_fusion.1 = f32[1,8,4,48,128]{4,3,2,1,0:T(8,128)S(1)} fusion(f32[8,4,48,768]{3,2,1,0:T(8,128)} %bitcast.53, f32[768,128,1,1]{1,0,3,2:T(8,128)S(1)} %bitcast.58), kind=kOutput, calls=%fused_computation.5 | convolution fusion | flops 905969664 | bytes 5898240 | tf_op jit(solution)/shard_map/dot_general | solution.py:46
  119.8 2.0 %convolution_bitcast_fusion = f32[1,8,4,48,128]{4,3,2,1,0:T(8,128)S(1)} fusion(f32[8,4,48,768]{3,2,1,0:T(8,128)S(1)} %bitcast.52, f32[768,128,1,1]{1,0,3,2:T(8,128)S(1)} %bitcast.59), kind=kOutput, calls=%fused_computation.4 | convolution fusion | flops 905969664 | bytes 5898240 | tf_op jit(solution)/shard_map/dot_general | solution.py:46
  122.1 21.6 %all_to_all.31 = f32[4,16,48,128]{3,2,1,0:T(8,128)S(1)} all-to-all(f32[4,16,48,128]{3,2,1,0:T(8,128)S(1)} %bitcast.57), channel_id=1, replica_groups=mesh['z'=8,'x'=4,'y'=8,'c'=2] {'x'}, dimensions={0} | all-to-all | bytes 3145728 | tf_op jit(solution)/shard_map/all_to_all | solution.py:67
  143.7 0.9 reduce_sum.28
  144.5 5.9 %all-to-all-start.5 = ((f32[16,48,128]{2,1,0:T(8,128)}), f32[16,48,128]{2,1,0:T(8,128)S(1)}, u32[]{:S(2)}, u32[]{:S(2)}) async-start(f32[16,48,128]{2,1,0:T(8,128)} %reduce_sum.28), calls=%async_computation.5 | async-start | bytes 786432 | tf_op jit(solution)/shard_map/all_to_all | solution.py:68
  150.4 2.1 %collective-permute-start.1 = (f32[48,128]{1,0:T(8,128)S(1)}, f32[48,128]{1,0:T(8,128)S(1)}, u32[]{:S(2)}, u32[]{:S(2)}) collective-permute-start(f32[48,128]{1,0:T(8,128)S(1)} %get-tuple-element.3), channel_id=1, source_target_pairs={{0,1},{1,0},{2,3},{3,2},{4,5},{5,4},{6,7},{7,6},{8,9},{9,8},{10,11... | collective-permute-start | bytes 73736 | tf_op jit(solution)/shard_map/ppermute | solution.py:60
  152.8 0.8 collective-permute-done.1
  153.5 0.6 maximum_select_fusion.1
  154.1 10.8 %all-to-all-done.5 = f32[16,48,128]{2,1,0:T(8,128)S(1)} async-done(((f32[16,48,128]{2,1,0:T(8,128)}), f32[16,48,128]{2,1,0:T(8,128)S(1)}, u32[]{:S(2)}, u32[]{:S(2)}) %all-to-all-start.5) | async-done | bytes 393248 | tf_op jit(solution)/shard_map/all_to_all | solution.py:68
  165.0 0.6 bitcast_subtract_fusion
  (24 shorter events, 1.2 us)
Async XLA Ops:
  0.6 15.0 %copy-start.3 = (f32[48,256]{1,0:T(8,128)S(1)}, f32[48,256]{1,0:T(8,128)}, u32[]{:S(2)}) copy-start(f32[48,256]{1,0:T(8,128)} %param.4) | copy-start | bytes 147460
  6.7 33.7 %copy-start.4 = (f32[3]{0:T(128)S(1)}, f32[3]{0:T(128)}, u32[]{:S(2)}) copy-start(f32[3]{0:T(128)} %param.5) | copy-start | bytes 40
  6.7 55.1 %collective-permute-start = (f32[768,1536]{0,1:T(8,128)}, f32[768,1536]{0,1:T(8,128)}, u32[]{:S(2)}, u32[]{:S(2)}) collective-permute-start(f32[768,1536]{0,1:T(8,128)} %copy.22), channel_id=1, source_target_pairs={{0,1},{1,0},{2,3},{3,2},{4,5},{5,4},{6,7},{7,6},{8,9},{9,8},{10,11... | collective-permute-start | bytes 14155784 | tf_op jit(solution)/shard_map/ppermute | solution.py:26
  36.4 25.2 %all-to-all-start.1 = ((f32[4,16,48,128]{3,2,1,0:T(8,128)}), f32[4,16,48,128]{3,2,1,0:T(8,128)S(1)}, u32[]{:S(2)}, u32[]{:S(2)}) async-start(f32[4,16,48,128]{3,2,1,0:T(8,128)} %broadcast_in_dim.7), calls=%async_computation.1 | async-start | bytes 3145728 | tf_op jit(solution)/shard_map/all_to_all | solution.py:40
  66.2 8.6 %copy-start = (f32[768,1536]{0,1:T(8,128)}, f32[768,1536]{0,1:T(8,128)S(1)}, u32[]{:S(2)}) copy-start(f32[768,1536]{0,1:T(8,128)S(1)} %get-tuple-element.4) | copy-start | bytes 14155780
  66.2 8.6 %copy-start.2 = (f32[768,1536]{0,1:T(8,128)}, f32[768,1536]{0,1:T(8,128)S(1)}, u32[]{:S(2)}) copy-start(f32[768,1536]{0,1:T(8,128)S(1)} %get-tuple-element.5) | copy-start | bytes 14155780
  74.8 22.0 %all-to-all-start.2 = ((f32[8,96,128]{2,1,0:T(8,128)}), f32[8,96,128]{2,1,0:T(8,128)S(1)}, u32[]{:S(2)}, u32[]{:S(2)}) async-start(f32[8,96,128]{2,1,0:T(8,128)} %bitcast.10), calls=%async_computation.2 | async-start | bytes 786432 | tf_op jit(solution)/shard_map/all_to_all | solution.py:52
  97.6 17.7 %all-to-all-start.3 = ((f32[8,96,128]{2,1,0:T(8,128)}), f32[8,96,128]{2,1,0:T(8,128)S(1)}, u32[]{:S(2)}, u32[]{:S(2)}) async-start(f32[8,96,128]{2,1,0:T(8,128)} %broadcast_in_dim.8), calls=%async_computation.3 | async-start | bytes 786432 | tf_op jit(solution)/shard_map/all_to_all | solution.py:55
  115.2 4.5 %copy-start.1 = (f32[768,1536]{0,1:T(8,128)S(1)}, f32[768,1536]{0,1:T(8,128)}, u32[]{:S(2)}) copy-start(f32[768,1536]{0,1:T(8,128)} %copy-done) | copy-start | bytes 14155780
  144.5 20.4 %all-to-all-start.5 = ((f32[16,48,128]{2,1,0:T(8,128)}), f32[16,48,128]{2,1,0:T(8,128)S(1)}, u32[]{:S(2)}, u32[]{:S(2)}) async-start(f32[16,48,128]{2,1,0:T(8,128)} %reduce_sum.28), calls=%async_computation.5 | async-start | bytes 786432 | tf_op jit(solution)/shard_map/all_to_all | solution.py:68
  150.4 3.1 %collective-permute-start.1 = (f32[48,128]{1,0:T(8,128)S(1)}, f32[48,128]{1,0:T(8,128)S(1)}, u32[]{:S(2)}, u32[]{:S(2)}) collective-permute-start(f32[48,128]{1,0:T(8,128)S(1)} %get-tuple-element.3), channel_id=1, source_target_pairs={{0,1},{1,0},{2,3},{3,2},{4,5},{5,4},{6,7},{7,6},{8,9},{9,8},{10,11... | collective-permute-start | bytes 73736 | tf_op jit(solution)/shard_map/ppermute | solution.py:60

commit v2 on v1

v2 whole, which is shorter than its diff:
```python
import jax
import jax.numpy as jnp
from jax import lax
from jax.experimental import pallas as pl
from jax.experimental.pallas import tpu as pltpu
from jax.sharding import Mesh, PartitionSpec as P

BF, F32 = jnp.bfloat16, jnp.float32
VMEM_LIMIT = 16 * 1024 * 1024


def split(v):
    hi = v.astype(BF)
    return hi, (v - hi.astype(F32)).astype(BF)


def split_kernel(place_ref, center_ref, mine_ref, theirs_ref, out_ref):
    rows, cols = mine_ref.shape
    core = place_ref[0]
    first_row = place_ref[1] + pl.program_id(0) * rows
    row = lax.broadcasted_iota(jnp.int32, (rows, cols), 0)
    col = lax.broadcasted_iota(jnp.int32, (rows, cols), 1)
    center = center_ref[0]
    for block, tile_ref in ((core, mine_ref), (1 - core, theirs_ref)):
        first_col = place_ref[2] + block * cols
        tile = tile_ref[...] - jnp.where(row + (first_row - first_col) == col, center, 0.0)
        hi, lo = split(tile)
        out_ref[block, 0] = hi
        out_ref[block, 1] = lo


def split_tiles(place, center, mine, theirs, step=128):
    rows, cols = mine.shape
    smem = pl.BlockSpec(memory_space=pltpu.SMEM)
    tile = pl.BlockSpec((step, cols), lambda i: (i, 0))
    return pl.pallas_call(
        split_kernel,
        grid=(rows // step,),
        in_specs=[smem, smem, tile, tile],
        out_specs=pl.BlockSpec((2, 2, step, cols), lambda i: (0, 0, i, 0)),
        out_shape=jax.ShapeDtypeStruct((2, 2, rows, cols), BF),
        compiler_params=pltpu.CompilerParams(vmem_limit_bytes=VMEM_LIMIT),
        cost_estimate=pl.CostEstimate(flops=8 * rows * cols, bytes_accessed=16 * rows * cols, transcendentals=0),
    )(place, center, mine, theirs)


def rows_kernel(h_ref, x_ref, out_ref, wide):
    xs, zc, piece, part = x_ref.shape

    @pl.when(pl.program_id(0) == 0)
    def _():
        for zi in range(zc // 2):
            for block in range(2):
                for xi in range(xs):
                    hi, lo = split(x_ref[xi, zi * 2 + block])
                    at = pl.ds((zi * xs + xi) * piece, piece)
                    wide[block, at, :part] = hi
                    wide[block, at, part:] = lo

    step, cols = h_ref.shape[2:]
    acc = jnp.dot(h_ref[0].reshape(2 * step, cols), wide[0], preferred_element_type=F32)
    acc += jnp.dot(h_ref[1].reshape(2 * step, cols), wide[1], preferred_element_type=F32)
    acc = acc[:, :part] + acc[:, part:]
    out_ref[...] = acc[:step] + acc[step:]


def rows_product(h, x, step=128):
    _, _, rows, cols = h.shape
    xs, zc, piece, part = x.shape
    return pl.pallas_call(
        rows_kernel,
        grid=(rows // step,),
        in_specs=[
            pl.BlockSpec((2, 2, step, cols), lambda i: (0, 0, i, 0)),
            pl.BlockSpec(x.shape, lambda i: (0, 0, 0, 0)),
        ],
        out_specs=pl.BlockSpec((step, part), lambda i: (i, 0)),
        out_shape=jax.ShapeDtypeStruct((rows, part), F32),
        scratch_shapes=[pltpu.VMEM((2, cols, 2 * part), BF)],
        compiler_params=pltpu.CompilerParams(vmem_limit_bytes=VMEM_LIMIT),
        cost_estimate=pl.CostEstimate(
            flops=16 * rows * cols * part, bytes_accessed=8 * rows * cols, transcendentals=0
        ),
    )(h, x)


def cols_kernel(h_ref, y_ref, out_ref, tall):
    xs, zs, _, piece, part = out_ref.shape

    @pl.when((pl.program_id(0) == 0) & (pl.program_id(1) == 0))
    def _():
        share = y_ref.shape[1]
        flat = y_ref[...].reshape(y_ref.shape[0] * share, part).T
        hi, lo = split(flat)
        tall[:part] = hi
        tall[part:] = lo

    acc = jnp.dot(tall[...], h_ref[0, 0], preferred_element_type=F32)
    acc += jnp.dot(tall[...], h_ref[0, 1], preferred_element_type=F32)
    out = (acc[:part] + acc[part:]).T
    for zi in range(zs):
        for xi in range(xs):
            at = (zi * xs + xi) * piece
            out_ref[xi, zi, 0] = out[at : at + piece]


def cols_product(h, y, xs, zs, steps=2):
    _, _, rows, cols = h.shape
    part = y.shape[-1]
    piece = cols // (xs * zs)
    return pl.pallas_call(
        cols_kernel,
        grid=(2, steps),
        in_specs=[
            pl.BlockSpec((1, 2, rows, cols // steps), lambda b, j: (b, 0, 0, j)),
            pl.BlockSpec(y.shape, lambda b, j: (0, 0, 0)),
        ],
        out_specs=pl.BlockSpec((xs, zs // steps, 1, piece, part), lambda b, j: (0, j, b, 0, 0)),
        out_shape=jax.ShapeDtypeStruct((xs, zs, 2, piece, part), F32),
        scratch_shapes=[pltpu.VMEM((2 * part, rows), BF)],
        compiler_params=pltpu.CompilerParams(vmem_limit_bytes=VMEM_LIMIT),
        cost_estimate=pl.CostEstimate(
            flops=16 * rows * cols * part, bytes_accessed=8 * rows * cols, transcendentals=0
        ),
    )(h, y)


def body(hamiltonian, search_block, filter_bounds):
    lower = filter_bounds[0]
    low_end = filter_bounds[1]
    high_end = filter_bounds[2]
    center = (high_end + low_end) / 2.0
    half = (high_end - low_end) / 2.0
    sigma_one = half / (lower - center)
    sigma_two = 1.0 / (2.0 / sigma_one - sigma_one)
    scale_one = sigma_one / half
    scale_two = 2.0 * sigma_two / half
    damp = sigma_two * sigma_one

    zs, xs, ys, cs = (lax.axis_size(a) for a in ("z", "x", "y", "c"))
    z, x, y, c = (lax.axis_index(a) for a in ("z", "x", "y", "c"))
    rows_tile, cols_tile = hamiltonian.shape
    piece, width = search_block.shape
    part = width // cs
    swap = [(i, cs - 1 - i) for i in range(cs)]

    other = lax.ppermute(hamiltonian, "c", swap)
    place = jnp.stack([c, (z * xs + x) * rows_tile, y * cs * cols_tile]).astype(jnp.int32)
    tiles = split_tiles(place, center.reshape(1), hamiltonian, other)

    halves = search_block.reshape(piece, cs, part).transpose(1, 0, 2)
    sent = jnp.broadcast_to(halves[None], (zs, cs, piece, part)).reshape(zs * cs, piece, part)
    got = lax.all_to_all(sent, ("z", "c"), 0, 0, tiled=True)
    sent = jnp.broadcast_to(got[None], (xs,) + got.shape)
    got = lax.all_to_all(sent, "x", 0, 0, tiled=True)

    partial_rows = rows_product(tiles, got)
    share = rows_tile // ys
    terms = lax.all_to_all(partial_rows.reshape(ys, share, part), "y", 0, 0, tiled=True)
    first = scale_one * terms.sum(0)
    sent = jnp.broadcast_to(first[None], (ys, share, part))
    first_rows = lax.all_to_all(sent, "y", 0, 0, tiled=True)

    first_pair = first.reshape(cs, piece, part)
    keep = lax.dynamic_index_in_dim(first_pair, c, 0, keepdims=False)
    give = lax.dynamic_index_in_dim(first_pair, cs - 1 - c, 0, keepdims=False)
    came = lax.ppermute(give, "c", swap)
    first_out = jnp.where(c == 0, jnp.concatenate([keep, came], 1), jnp.concatenate([came, keep], 1))

    sent = cols_product(tiles, first_rows, xs, zs).reshape(xs, zs * cs, piece, part)
    summed = lax.all_to_all(sent, "x", 0, 0, tiled=True).sum(0)
    summed = lax.all_to_all(summed, ("z", "c"), 0, 0, tiled=True)
    summed = summed.reshape(zs, cs, piece, part).sum(0).transpose(1, 0, 2).reshape(piece, width)
    second_out = scale_two * summed - damp * search_block
    return (first_out, second_out)


def solution(mesh):
    fine = Mesh(mesh.devices.reshape(8, 4, 8, 2), ("z", "x", "y", "c"))
    row, col = ("z", "x"), ("y", "c")
    return jax.shard_map(
        body,
        mesh=fine,
        in_specs=(P(row, col), P(col + row, None), P()),
        out_specs=(P(row + col, None), P(col + row, None)),
        check_vma=False,
    )
```

time: 166 us -> 156 us (0.940)
  waiting for transfers between devices: 58.1 us -> 32.3 us
  blocking collectives: 41 us -> 57.7 us
  Pallas kernels: 0 us -> 15.3 us
  matrix products: 15.1 us -> 0 us
  local copies, waits for them, and re-layouts: 9.12 us -> 16.1 us
  other arithmetic: 6.71 us -> 2.24 us
  starting transfers between devices: 31.4 us -> 27.8 us
    all_to_all x0 -> x1, blocking collectives: none -> 16.7 us  [body(): first_rows = lax.all_to_all(sent, 'y', 0, 0, tiled=True)]
    pallas_call x0 -> x3, Pallas kernels: none -> 15.3 us  [the longest x1 5.81 us: split_tiles(): pl.pallas_call(split_kernel, grid=(rows // step,), in_specs=[smem, smem,...]
    dot_general x4 -> x0, matrix products: 15.1 us -> none  [dot(): lax.dot_general(a, b, (dims, ((), ())), precision=lax.Precision.HIGH, pre...]
    all_to_all x1 -> x0, waiting for transfers between devices: 14 us -> none  [body(): lax.all_to_all(sent, 'y', 0, 0, tiled=True).reshape(rows_tile, part)]
    all_to_all x1, waiting for transfers between devices: 19.3 us -> 7.52 us  [body(): got = lax.all_to_all(sent, 'x', 0, 0, tiled=True)]
    unnamed x11 -> x12, local copies, waits for them, and re-layouts: 6.09 us -> 13.3 us
    sub x1 -> x0, other arithmetic: 4.4 us -> none  [shift(): return tile - center * (global_rows == global_cols).astype(jnp.float32)]
    all_to_all x1 -> x0, starting transfers between devices: 3.63 us -> none  [body(): lax.all_to_all(sent, 'y', 0, 0, tiled=True).reshape(rows_tile, part)]
  transfers between devices with their start and end apart: 6 -> 5, of which waited for: 5 -> 4; matrix products, arithmetic and copies ran while one was open for 2% -> 2% of each run, Pallas kernels for 0% -> 4%
where the time goes in v2:
time: 156 us
  blocking collectives  57.7 us (37%)
  waiting for transfers between devices  32.3 us (21%)
  starting transfers between devices  27.8 us (18%)
  local copies, waits for them, and re-layouts  16.1 us (10%)
  Pallas kernels  15.3 us (10%)
  between operations  4.06 us (3%)
  other arithmetic  2.24 us (1%)
    all_to_all x1, blocking collectives, body(): summed = lax.all_to_all(sent, 'x', 0, 0, tiled=True).sum(0)  21.6 us
    all_to_all x1, blocking collectives, body(): got = lax.all_to_all(sent, ('z', 'c'), 0, 0, tiled=True)  19.4 us
    all_to_all x1, blocking collectives, body(): first_rows = lax.all_to_all(sent, 'y', 0, 0, tiled=True)  16.7 us
    unnamed x12, local copies, waits for them, and re-layouts  13.3 us
    all_to_all x1, waiting for transfers between devices, body(): lax.all_to_all(partial_rows.reshape(ys, share, part), 'y', 0, 0, tiled=True)  13.2 us
    all_to_all x1, waiting for transfers between devices, body(): summed = lax.all_to_all(summed, ('z', 'c'), 0, 0, tiled=True)  10.8 us
    ppermute x1, starting transfers between devices, body(): other = lax.ppermute(hamiltonian, 'c', swap)  8.79 us
    all_to_all x1, waiting for transfers between devices, body(): got = lax.all_to_all(sent, 'x', 0, 0, tiled=True)  7.52 us
  transfers between devices with their start and end apart: 5, of which 4 were waited for; matrix products, arithmetic and copies ran while one was open for 2% of the time, Pallas kernels for 4%

profile of v2, /device:TPU:1, one launch (start us, length us, event | category | flops | bytes accessed | tf_op | source)
XLA Modules:
  0.0 155.5 jit_solution(2963749545220030037)
XLA Ops:
  0.6 8.8 %collective-permute-start = (f32[768,1536]{1,0:T(8,128)}, f32[768,1536]{1,0:T(8,128)}, u32[]{:S(2)}, u32[]{:S(2)}) collective-permute-start(f32[768,1536]{1,0:T(8,128)} %mine_ref.1), channel_id=1, source_target_pairs={{0,1},{1,0},{2,3},{3,2},{4,5},{5,4},{6,7},{7,6},{8,9},{9,8},{10,11... | collective-permute-start | bytes 14155784 | tf_op jit(solution)/shard_map/ppermute | solution.py:147
  9.4 0.8 reshape.40
  10.3 19.4 %all_to_all.30 = f32[16,48,128]{2,1,0:T(8,128)S(1)} all-to-all(f32[16,48,128]{2,1,0:T(8,128)S(1)} %bitcast.23), channel_id=1, replica_groups=mesh['z'=8,'x'=4,'y'=8,'c'=2] {'z','c'}, dimensions={0} | all-to-all | bytes 786432 | tf_op jit(solution)/shard_map/all_to_all | solution.py:153
  29.7 1.3 broadcast_in_dim.7
  31.0 4.1 %all-to-all-start.1 = ((f32[4,16,48,128]{3,2,1,0:T(8,128)}), f32[4,16,48,128]{3,2,1,0:T(8,128)S(1)}, u32[]{:S(2)}, u32[]{:S(2)}) async-start(f32[4,16,48,128]{3,2,1,0:T(8,128)} %broadcast_in_dim.7), calls=%async_computation.1 | async-start | bytes 3145728 | tf_op jit(solution)/shard_map/all_to_all | solution.py:155
  37.1 2.3 %copy-done.3 = f32[768,1536]{1,0:T(8,128)S(1)} copy-done((f32[768,1536]{1,0:T(8,128)S(1)}, f32[768,1536]{1,0:T(8,128)}, u32[]{:S(2)}) %copy-start.3) | copy-done | bytes 4718616
  39.4 5.8 %shard_map.50.h_ref = bf16[2,2,768,1536]{3,2,1,0:T(8,128)(2,1)S(1)} custom-call(s32[3]{0:T(128)S(1)} %pad_add_fusion.place_ref, f32[1]{0:T(128)S(6)} %div.25.center_ref, f32[768,1536]{1,0:T(8,128)S(1)} %copy-done.3, f32[768,1536]{1,0:T(8,128)} %collective-permute-done.theirs_ref), custom_call_target="tpu_custom_call" | custom-call | flops 9437184 | bytes 18874368 | tf_op jit(solution)/shard_map/pallas_call | solution.py:36
  45.2 3.6 %copy-done = bf16[2,2,768,1536]{3,2,1,0:T(8,128)(2,1)} copy-done((bf16[2,2,768,1536]{3,2,1,0:T(8,128)(2,1)}, bf16[2,2,768,1536]{3,2,1,0:T(8,128)(2,1)S(1)}, u32[]{:S(2)}) %copy-start) | copy-done | bytes 9437208
  48.9 7.5 %all-to-all-done.1.x_ref = f32[4,16,48,128]{3,2,1,0:T(8,128)S(1)} async-done(((f32[4,16,48,128]{3,2,1,0:T(8,128)}), f32[4,16,48,128]{3,2,1,0:T(8,128)S(1)}, u32[]{:S(2)}, u32[]{:S(2)}) %all-to-all-start.1) | async-done | bytes 1572896 | tf_op jit(solution)/shard_map/all_to_all | solution.py:155
  56.4 3.7 %copy-done.1 = bf16[2,2,768,1536]{3,2,1,0:T(8,128)(2,1)S(1)} copy-done((bf16[2,2,768,1536]{3,2,1,0:T(8,128)(2,1)S(1)}, bf16[2,2,768,1536]{3,2,1,0:T(8,128)(2,1)}, u32[]{:S(2)}) %copy-start.1) | copy-done | bytes 9437208
  60.1 5.1 %shard_map.51 = f32[768,128]{1,0:T(8,128)} custom-call(bf16[2,2,768,1536]{3,2,1,0:T(8,128)(2,1)S(1)} %copy-done.1, f32[4,16,48,128]{3,2,1,0:T(8,128)S(1)} %all-to-all-done.1.x_ref), custom_call_target="tpu_custom_call" | custom-call | flops 2415919104 | bytes 9437184 | tf_op jit(solution)/shard_map/pallas_call | solution.py:70
  65.1 6.8 %all-to-all-start.2 = ((f32[8,96,128]{2,1,0:T(8,128)}), f32[8,96,128]{2,1,0:T(8,128)S(1)}, u32[]{:S(2)}, u32[]{:S(2)}) async-start(f32[8,96,128]{2,1,0:T(8,128)} %bitcast.7), calls=%async_computation.2 | async-start | bytes 786432 | tf_op jit(solution)/shard_map/all_to_all | solution.py:159
  73.9 13.2 %all-to-all-done.2 = f32[8,96,128]{2,1,0:T(8,128)S(1)} async-done(((f32[8,96,128]{2,1,0:T(8,128)}), f32[8,96,128]{2,1,0:T(8,128)S(1)}, u32[]{:S(2)}, u32[]{:S(2)}) %all-to-all-start.2) | async-done | bytes 393248 | tf_op jit(solution)/shard_map/all_to_all | solution.py:159
  87.2 16.7 %all_to_all.31.y_ref = f32[8,96,128]{2,1,0:T(8,128)S(1)} all-to-all(f32[8,96,128]{2,1,0:T(8,128)S(1)} %broadcast_in_dim.8), channel_id=1, replica_groups=mesh['z'=8,'x'=4,'y'=8,'c'=2] {'y'}, dimensions={0} | all-to-all | bytes 786432 | tf_op jit(solution)/shard_map/all_to_all | solution.py:162
  103.9 3.7 %copy-done.2 = bf16[2,2,768,1536]{3,2,1,0:T(8,128)(2,1)S(1)} copy-done((bf16[2,2,768,1536]{3,2,1,0:T(8,128)(2,1)S(1)}, bf16[2,2,768,1536]{3,2,1,0:T(8,128)(2,1)}, u32[]{:S(2)}) %copy-start.2) | copy-done | bytes 9437208
  107.5 4.5 %shard_map.52 = f32[4,8,2,48,128]{4,3,2,1,0:T(8,128)S(1)} custom-call(bf16[2,2,768,1536]{3,2,1,0:T(8,128)(2,1)S(1)} %copy-done.2, f32[8,96,128]{2,1,0:T(8,128)S(1)} %all_to_all.31.y_ref), custom_call_target="tpu_custom_call" | custom-call | flops 2415919104 | bytes 9437184 | tf_op jit(solution)/shard_map/pallas_call | solution.py:111
  112.0 21.6 %all_to_all.32 = f32[4,16,48,128]{3,2,1,0:T(8,128)S(1)} all-to-all(f32[4,16,48,128]{3,2,1,0:T(8,128)S(1)} %bitcast.21), channel_id=1, replica_groups=mesh['z'=8,'x'=4,'y'=8,'c'=2] {'x'}, dimensions={0} | all-to-all | bytes 3145728 | tf_op jit(solution)/shard_map/all_to_all | solution.py:171
  133.6 0.9 reduce_sum.28
  134.4 5.9 %all-to-all-start.5 = ((f32[16,48,128]{2,1,0:T(8,128)}), f32[16,48,128]{2,1,0:T(8,128)S(1)}, u32[]{:S(2)}, u32[]{:S(2)}) async-start(f32[16,48,128]{2,1,0:T(8,128)} %reduce_sum.28), calls=%async_computation.5 | async-start | bytes 786432 | tf_op jit(solution)/shard_map/all_to_all | solution.py:172
  140.3 2.1 %collective-permute-start.1 = (f32[48,128]{1,0:T(8,128)S(1)}, f32[48,128]{1,0:T(8,128)S(1)}, u32[]{:S(2)}, u32[]{:S(2)}) collective-permute-start(f32[48,128]{1,0:T(8,128)S(1)} %get-tuple-element.3), channel_id=1, source_target_pairs={{0,1},{1,0},{2,3},{3,2},{4,5},{5,4},{6,7},{7,6},{8,9},{9,8},{10,11... | collective-permute-start | bytes 73736 | tf_op jit(solution)/shard_map/ppermute | solution.py:167
  142.7 0.8 collective-permute-done.1
  143.4 0.6 maximum_select_fusion
  144.0 10.8 %all-to-all-done.5 = f32[16,48,128]{2,1,0:T(8,128)S(1)} async-done(((f32[16,48,128]{2,1,0:T(8,128)}), f32[16,48,128]{2,1,0:T(8,128)S(1)}, u32[]{:S(2)}, u32[]{:S(2)}) %all-to-all-start.5) | async-done | bytes 393248 | tf_op jit(solution)/shard_map/all_to_all | solution.py:172
  154.9 0.6 bitcast_subtract_fusion
  (18 shorter events, 0.8 us)
Async XLA Ops:
  0.6 36.4 %collective-permute-start = (f32[768,1536]{1,0:T(8,128)}, f32[768,1536]{1,0:T(8,128)}, u32[]{:S(2)}, u32[]{:S(2)}) collective-permute-start(f32[768,1536]{1,0:T(8,128)} %mine_ref.1), channel_id=1, source_target_pairs={{0,1},{1,0},{2,3},{3,2},{4,5},{5,4},{6,7},{7,6},{8,9},{9,8},{10,11... | collective-permute-start | bytes 14155784 | tf_op jit(solution)/shard_map/ppermute | solution.py:147
  31.0 4.1 %copy-start.5 = (f32[3]{0:T(128)S(1)}, f32[3]{0:T(128)}, u32[]{:S(2)}) copy-start(f32[3]{0:T(128)} %param.5) | copy-start | bytes 40
  31.0 25.4 %all-to-all-start.1 = ((f32[4,16,48,128]{3,2,1,0:T(8,128)}), f32[4,16,48,128]{3,2,1,0:T(8,128)S(1)}, u32[]{:S(2)}, u32[]{:S(2)}) async-start(f32[4,16,48,128]{3,2,1,0:T(8,128)} %broadcast_in_dim.7), calls=%async_computation.1 | async-start | bytes 3145728 | tf_op jit(solution)/shard_map/all_to_all | solution.py:155
  37.1 2.3 %copy-start.3 = (f32[768,1536]{1,0:T(8,128)S(1)}, f32[768,1536]{1,0:T(8,128)}, u32[]{:S(2)}) copy-start(f32[768,1536]{1,0:T(8,128)} %mine_ref.1) | copy-start | bytes 14155780
  45.2 3.6 %copy-start = (bf16[2,2,768,1536]{3,2,1,0:T(8,128)(2,1)}, bf16[2,2,768,1536]{3,2,1,0:T(8,128)(2,1)S(1)}, u32[]{:S(2)}) copy-start(bf16[2,2,768,1536]{3,2,1,0:T(8,128)(2,1)S(1)} %shard_map.50.h_ref) | copy-start | bytes 28311556
  56.4 3.7 %copy-start.1 = (bf16[2,2,768,1536]{3,2,1,0:T(8,128)(2,1)S(1)}, bf16[2,2,768,1536]{3,2,1,0:T(8,128)(2,1)}, u32[]{:S(2)}) copy-start(bf16[2,2,768,1536]{3,2,1,0:T(8,128)(2,1)} %copy-done) | copy-start | bytes 28311556
  65.1 22.0 %all-to-all-start.2 = ((f32[8,96,128]{2,1,0:T(8,128)}), f32[8,96,128]{2,1,0:T(8,128)S(1)}, u32[]{:S(2)}, u32[]{:S(2)}) async-start(f32[8,96,128]{2,1,0:T(8,128)} %bitcast.7), calls=%async_computation.2 | async-start | bytes 786432 | tf_op jit(solution)/shard_map/all_to_all | solution.py:159
  103.9 3.7 %copy-start.2 = (bf16[2,2,768,1536]{3,2,1,0:T(8,128)(2,1)S(1)}, bf16[2,2,768,1536]{3,2,1,0:T(8,128)(2,1)}, u32[]{:S(2)}) copy-start(bf16[2,2,768,1536]{3,2,1,0:T(8,128)(2,1)} %copy-done) | copy-start | bytes 28311556
  133.6 21.3 %copy-start.4 = (f32[48,256]{1,0:T(8,128)S(1)}, f32[48,256]{1,0:T(8,128)}, u32[]{:S(2)}) copy-start(f32[48,256]{1,0:T(8,128)} %param.4) | copy-start | bytes 147460
  134.4 20.4 %all-to-all-start.5 = ((f32[16,48,128]{2,1,0:T(8,128)}), f32[16,48,128]{2,1,0:T(8,128)S(1)}, u32[]{:S(2)}, u32[]{:S(2)}) async-start(f32[16,48,128]{2,1,0:T(8,128)} %reduce_sum.28), calls=%async_computation.5 | async-start | bytes 786432 | tf_op jit(solution)/shard_map/all_to_all | solution.py:172
  140.3 3.1 %collective-permute-start.1 = (f32[48,128]{1,0:T(8,128)S(1)}, f32[48,128]{1,0:T(8,128)S(1)}, u32[]{:S(2)}, u32[]{:S(2)}) collective-permute-start(f32[48,128]{1,0:T(8,128)S(1)} %get-tuple-element.3), channel_id=1, source_target_pairs={{0,1},{1,0},{2,3},{3,2},{4,5},{5,4},{6,7},{7,6},{8,9},{9,8},{10,11... | collective-permute-start | bytes 73736 | tf_op jit(solution)/shard_map/ppermute | solution.py:167

commit v3 on v1

v3 whole, which is shorter than its diff:
```python
import jax
import jax.numpy as jnp
from jax import lax
from jax.experimental import pallas as pl
from jax.experimental.pallas import tpu as pltpu
from jax.sharding import Mesh, PartitionSpec as P

BF, F32 = jnp.bfloat16, jnp.float32
SMEM = pl.BlockSpec(memory_space=pltpu.SMEM)
VMEM = pl.BlockSpec(memory_space=pltpu.VMEM)
HBM = pl.BlockSpec(memory_space=pl.ANY)
AHEAD = 3
PARAMS = pltpu.CompilerParams(vmem_limit_bytes=60 * 1024 * 1024)


def split(v):
    hi = v.astype(BF)
    return hi, (v - hi.astype(F32)).astype(BF)


def deal_kernel(search_ref, out_ref):
    part = out_ref.shape[-1]
    for zi in range(out_ref.shape[0]):
        for ci in range(out_ref.shape[1]):
            out_ref[zi, ci] = search_ref[:, ci * part : (ci + 1) * part]


def split_kernel(place_ref, bounds_ref, mine_ref, theirs_ref, mine_out, theirs_out, scalars_ref):
    rows, cols = mine_ref.shape
    center = (bounds_ref[2] + bounds_ref[1]) / 2.0
    row = lax.broadcasted_iota(jnp.int32, (rows, cols), 0)
    col = lax.broadcasted_iota(jnp.int32, (rows, cols), 1)
    apart = col - row
    for t, (tile_ref, out_ref) in enumerate(((mine_ref, mine_out), (theirs_ref, theirs_out))):
        offset = place_ref[t] + pl.program_id(0) * rows
        hi, lo = split(tile_ref[...] - jnp.where(apart == offset, center, 0.0))
        out_ref[0] = hi
        out_ref[1] = lo

    @pl.when(pl.program_id(0) == 0)
    def _():
        lower, low_end, high_end = (jnp.full((1, scalars_ref.shape[1]), bounds_ref[i], F32) for i in range(3))
        center = (high_end + low_end) / 2.0
        half = (high_end - low_end) / 2.0
        sigma_one = half / (lower - center)
        sigma_two = 1.0 / (2.0 / sigma_one - sigma_one)
        scalars_ref[0:1] = sigma_one / half
        scalars_ref[1:2] = 2.0 * sigma_two / half
        scalars_ref[2:3] = sigma_two * sigma_one


def split_tiles(offsets, bounds, mine, theirs, width, step=256):
    rows, cols = mine.shape
    tile = pl.BlockSpec((step, cols), lambda i: (i, 0))
    out = pl.BlockSpec((2, step, cols), lambda i: (0, i, 0))
    return pl.pallas_call(
        split_kernel,
        grid=(rows // step,),
        in_specs=[SMEM, SMEM, tile, tile],
        out_specs=(out, out, pl.BlockSpec((8, width), lambda i: (0, 0))),
        out_shape=(
            jax.ShapeDtypeStruct((2, rows, cols), BF),
            jax.ShapeDtypeStruct((2, rows, cols), BF),
            jax.ShapeDtypeStruct((8, width), F32),
        ),
        compiler_params=PARAMS,
        cost_estimate=pl.CostEstimate(flops=16 * rows * cols, bytes_accessed=16 * rows * cols, transcendentals=0),
    )(offsets, bounds, mine, theirs)


def stream(copies, ahead):
    for copy in copies[:ahead]:
        copy.start()
    yield
    for i, copy in enumerate(copies):
        copy.wait()
        if i + ahead < len(copies):
            copies[i + ahead].start()
        yield


def rows_kernel(core_ref, mine_ref, theirs_ref, x_ref, out_ref, tiles, wide, sems):
    outer, inner, piece, part = x_ref.shape
    steps, step, cols = tiles.shape[1], tiles.shape[3], tiles.shape[4]
    landed = stream(
        [
            pltpu.make_async_copy(ref.at[:, pl.ds(i * step, step), :], tiles.at[t, i], sems.at[t, i])
            for i in range(steps)
            for t, ref in enumerate((mine_ref, theirs_ref))
        ],
        AHEAD,
    )
    next(landed)
    for t in range(2):
        block = core_ref[0] if t == 0 else 1 - core_ref[0]
        for zi in range(inner // 2):
            for xi in range(outer):
                hi, lo = split(x_ref[xi, zi * 2 + block])
                at = pl.ds((zi * outer + xi) * piece, piece)
                wide[t, at, :part] = hi
                wide[t, at, part:] = lo
    for i in range(steps):
        acc = None
        for t in range(2):
            next(landed)
            term = jnp.dot(tiles[t, i].reshape(2 * step, cols), wide[t], preferred_element_type=F32)
            acc = term if acc is None else acc + term
        acc = acc[:, :part] + acc[:, part:]
        out_ref[pl.ds(i * step, step), :] = acc[:step] + acc[step:]


def rows_product(core, mine, theirs, x, step=256):
    _, rows, cols = mine.shape
    part = x.shape[-1]
    return pl.pallas_call(
        rows_kernel,
        in_specs=[SMEM, HBM, HBM, VMEM],
        out_specs=VMEM,
        out_shape=jax.ShapeDtypeStruct((rows, part), F32),
        scratch_shapes=[
            pltpu.VMEM((2, rows // step, 2, step, cols), BF),
            pltpu.VMEM((2, cols, 2 * part), BF),
            pltpu.SemaphoreType.DMA((2, rows // step)),
        ],
        compiler_params=PARAMS,
        cost_estimate=pl.CostEstimate(
            flops=16 * rows * cols * part, bytes_accessed=8 * rows * cols, transcendentals=0
        ),
    )(core, mine, theirs, x)


def cols_kernel(core_ref, mine_ref, theirs_ref, y_ref, out_ref, tiles, tall, sems):
    outer, _, piece, part = out_ref.shape
    steps, depths, depth, step = tiles.shape[1], tiles.shape[2], tiles.shape[4], tiles.shape[5]
    landed = stream(
        [
            pltpu.make_async_copy(
                ref.at[:, pl.ds(k * depth, depth), pl.ds(i * step, step)], tiles.at[t, i, k], sems.at[t, i, k]
            )
            for i in range(steps)
            for t, ref in enumerate((mine_ref, theirs_ref))
            for k in range(depths)
        ],
        AHEAD,
    )
    next(landed)
    hi, lo = split(y_ref[...].reshape(-1, part).T)
    tall[:part] = hi
    tall[part:] = lo
    for i in range(steps):
        for t in range(2):
            block = core_ref[0] if t == 0 else 1 - core_ref[0]
            acc = None
            for k in range(depths):
                next(landed)
                for half in range(2):
                    term = jnp.dot(
                        tall[:, k * depth : (k + 1) * depth], tiles[t, i, k, half], preferred_element_type=F32
                    )
                    acc = term if acc is None else acc + term
            out = (acc[:part] + acc[part:]).T
            for p in range(step // piece):
                zi, xi = divmod(i * (step // piece) + p, outer)
                out_ref[xi, zi * 2 + block] = out[p * piece : (p + 1) * piece]


def cols_product(core, mine, theirs, y, outer, piece, step=768, depth=384):
    _, rows, cols = mine.shape
    part = y.shape[-1]
    return pl.pallas_call(
        cols_kernel,
        in_specs=[SMEM, HBM, HBM, VMEM],
        out_specs=VMEM,
        out_shape=jax.ShapeDtypeStruct((outer, 2 * cols // (outer * piece), piece, part), F32),
        scratch_shapes=[
            pltpu.VMEM((2, cols // step, rows // depth, 2, depth, step), BF),
            pltpu.VMEM((2 * part, rows), BF),
            pltpu.SemaphoreType.DMA((2, cols // step, rows // depth)),
        ],
        compiler_params=PARAMS,
        cost_estimate=pl.CostEstimate(
            flops=16 * rows * cols * part, bytes_accessed=8 * rows * cols, transcendentals=0
        ),
    )(core, mine, theirs, y)


def body(hamiltonian, search_block, filter_bounds):
    z2s, z1s, xs, ys, cs = (lax.axis_size(a) for a in ("z2", "z1", "x", "y", "c"))
    z2, z1, x, y, c = (lax.axis_index(a) for a in ("z2", "z1", "x", "y", "c"))
    rows_tile, cols_tile = hamiltonian.shape
    piece, width = search_block.shape
    part = width // cs
    outer = z1s * xs
    swap = [(i, cs - 1 - i) for i in range(cs)]
    core = c.reshape(1).astype(jnp.int32)

    first_row = ((z2 * z1s + z1) * xs + x) * rows_tile
    first_col = y * cs * cols_tile
    other = lax.ppermute(hamiltonian, "c", swap)
    offsets = (first_row - first_col - jnp.stack([c, cs - 1 - c]) * cols_tile).astype(jnp.int32)
    mine, theirs, scalars = split_tiles(offsets, filter_bounds, hamiltonian, other, width)

    sent = pl.pallas_call(deal_kernel, out_shape=jax.ShapeDtypeStruct((z2s, cs, piece, part), F32))(search_block)
    got = lax.all_to_all(sent.reshape(z2s * cs, piece, part), ("z2", "c"), 0, 0, tiled=True)
    got, mine, theirs, scalars = lax.optimization_barrier((got, mine, theirs, scalars))
    scale_one, scale_two, damp = scalars[0, :part], scalars[1, :part], scalars[2]
    sent = jnp.broadcast_to(got[None], (outer,) + got.shape)
    got = lax.all_to_all(sent, ("z1", "x"), 0, 0, tiled=True)

    partial_rows = rows_product(core, mine, theirs, got)
    share = rows_tile // ys
    terms = lax.all_to_all(partial_rows.reshape(ys, share, part), "y", 0, 0, tiled=True)
    first = scale_one * terms.sum(0)
    sent = jnp.broadcast_to(first[None], terms.shape)
    first_rows = lax.all_to_all(sent, "y", 0, 0, tiled=True)

    first_pair = first.reshape(cs, piece, part)
    keep = lax.dynamic_index_in_dim(first_pair, c, 0, keepdims=False)
    give = lax.dynamic_index_in_dim(first_pair, cs - 1 - c, 0, keepdims=False)
    came = lax.ppermute(give, "c", swap)
    first_out = jnp.where(c == 0, jnp.concatenate([keep, came], 1), jnp.concatenate([came, keep], 1))

    sent = cols_product(core, mine, theirs, first_rows, outer, piece)
    summed = lax.all_to_all(sent, ("z1", "x"), 0, 0, tiled=True).sum(0)
    summed = lax.all_to_all(summed, ("z2", "c"), 0, 0, tiled=True)
    summed = scale_two * summed.reshape(z2s, cs, piece, part).sum(0)
    second_out = summed.transpose(1, 0, 2).reshape(piece, width) - damp * search_block
    return (first_out, second_out)


def solution(mesh):
    fine = Mesh(mesh.devices.reshape(4, 2, 4, 8, 2), ("z2", "z1", "x", "y", "c"))
    row, col = ("z2", "z1", "x"), ("y", "c")
    return jax.shard_map(
        body,
        mesh=fine,
        in_specs=(P(row, col), P(col + row, None), P()),
        out_specs=(P(row + col, None), P(col + row, None)),
        check_vma=False,
    )
```

time: 166 us -> 150 us (0.904)
  Pallas kernels: 0 us -> 30.8 us
  waiting for transfers between devices: 58.1 us -> 33.9 us
  matrix products: 15.1 us -> 0 us
  starting transfers between devices: 31.4 us -> 41.1 us
  local copies, waits for them, and re-layouts: 9.12 us -> 1.64 us
  other arithmetic: 6.71 us -> 2.72 us
  between operations: 4.27 us -> 0.73 us
  blocking collectives: 41 us -> 38 us
    pallas_call x0 -> x4, Pallas kernels: none -> 30.8 us  [the longest x1 10.9 us: cols_product(): pl.pallas_call(cols_kernel, in_specs=[SMEM, HBM, HBM, VMEM], out_specs=VM...]
    all_to_all x3, waiting for transfers between devices: 44.1 us -> 22.1 us  [the longest x1 15.8 us: body(): summed = lax.all_to_all(sent, ('z1', 'x'), 0, 0, tiled=True).sum(0)]
    dot_general x4 -> x0, matrix products: 15.1 us -> none  [dot(): lax.dot_general(a, b, (dims, ((), ())), precision=lax.Precision.HIGH, pre...]
    all_to_all x3, starting transfers between devices: 13.5 us -> 23.6 us  [the longest x1 13.6 us: body(): summed = lax.all_to_all(summed, ('z2', 'c'), 0, 0, tiled=True)]
    unnamed x11 -> x2, local copies, waits for them, and re-layouts: 6.09 us -> 0.01 us
    sub x2, other arithmetic: 5.03 us -> 1.28 us  [the longest x1 0.65 us: body(): first_row - first_col - jnp.stack([c, cs - 1 - c]) * cols_tile]
    all_to_all x2, blocking collectives: 41 us -> 38 us  [the longest x1 24.2 us: body(): got = lax.all_to_all(sent, ('z1', 'x'), 0, 0, tiled=True)]
    all_to_all x1, waiting for transfers between devices: 13.2 us -> 10.7 us  [body(): lax.all_to_all(partial_rows.reshape(ys, share, part), 'y', 0, 0, tiled=True)]
  transfers between devices with their start and end apart: 6 -> 6, of which waited for: 5 -> 5; matrix products, arithmetic and copies ran while one was open for 2% -> 2% of each run, Pallas kernels for 0% -> 7%
where the time goes in v3:
time: 150 us; the launch traced here: 149 us
  starting transfers between devices  41.1 us (27%)
  blocking collectives  38 us (25%)
  waiting for transfers between devices  33.9 us (23%)
  Pallas kernels  30.8 us (21%)
  other arithmetic  2.72 us (2%)
  local copies, waits for them, and re-layouts  1.64 us (1%)
    all_to_all x1, blocking collectives, body(): got = lax.all_to_all(sent, ('z1', 'x'), 0, 0, tiled=True)  24.2 us
    all_to_all x1, waiting for transfers between devices, body(): summed = lax.all_to_all(sent, ('z1', 'x'), 0, 0, tiled=True).sum(0)  15.8 us
    all_to_all x1, blocking collectives, body(): first_rows = lax.all_to_all(sent, 'y', 0, 0, tiled=True)  13.9 us
    all_to_all x1, starting transfers between devices, body(): summed = lax.all_to_all(summed, ('z2', 'c'), 0, 0, tiled=True)  13.6 us
    pallas_call x1, Pallas kernels, cols_product(): pl.pallas_call(cols_kernel, in_specs=[SMEM, HBM, HBM, VMEM], out_specs=VM...  10.9 us
    all_to_all x1, waiting for transfers between devices, body(): lax.all_to_all(partial_rows.reshape(ys, share, part), 'y', 0, 0, tiled=True)  10.7 us
    pallas_call x1, Pallas kernels, split_tiles(): pl.pallas_call(split_kernel, grid=(rows // step,), in_specs=[SMEM, SMEM,...  9.45 us
    pallas_call x1, Pallas kernels, rows_product(): pl.pallas_call(rows_kernel, in_specs=[SMEM, HBM, HBM, VMEM], out_specs=VM...  9.01 us
  transfers between devices with their start and end apart: 6, of which 5 were waited for; matrix products, arithmetic and copies ran while one was open for 2% of the time, Pallas kernels for 7%

profile of v3, /device:TPU:1, one launch (start us, length us, event | category | flops | bytes accessed | tf_op | source)
XLA Modules:
  0.0 149.0 jit_solution(12754968849390668881)
XLA Ops:
  0.6 8.8 %collective-permute-start = (f32[768,1536]{1,0:T(8,128)}, f32[768,1536]{1,0:T(8,128)}, u32[]{:S(2)}, u32[]{:S(2)}) collective-permute-start(f32[768,1536]{1,0:T(8,128)} %mine_ref.1), channel_id=1, source_target_pairs={{0,1},{1,0},{2,3},{3,2},{4,5},{5,4},{6,7},{7,6},{8,9},{9,8},{10,11... | collective-permute-start | bytes 14155784 | tf_op jit(solution)/shard_map/ppermute | solution.py:199
  9.4 1.5 shard_map.50
  10.9 5.0 %all-to-all-start = ((f32[8,48,128]{2,1,0:T(8,128)}), f32[8,48,128]{2,1,0:T(8,128)S(1)}, u32[]{:S(2)}, u32[]{:S(2)}) async-start(f32[8,48,128]{2,1,0:T(8,128)} %bitcast.22), calls=%async_computation | async-start | bytes 393216 | tf_op jit(solution)/shard_map/all_to_all | solution.py:204
  15.9 0.7 fusion.place_ref
  16.6 0.7 collective-permute-done.theirs_ref
  17.3 9.4 %shard_map.51 = (bf16[2,768,1536]{2,1,0:T(8,128)(2,1)}, bf16[2,768,1536]{2,1,0:T(8,128)(2,1)}, f32[8,256]{1,0:T(8,128)}) custom-call(s32[2]{0:T(128)} %fusion.place_ref, f32[3]{0:T(128)} %bounds_ref.1, f32[768,1536]{1,0:T(8,128)} %mine_ref.1, f32[768,1536]{1,0:T(8,128)} %collective-permute-done.theirs_ref), custom_call_target="tpu_custom_call" | custom-call | flops 18874368 | bytes 18874368 | tf_op jit(solution)/shard_map/pallas_call | solution.py:56
  26.7 0.1 broadcast_in_dim.4
  26.9 24.2 %all_to_all.30.x_ref = f32[8,8,48,128]{3,2,1,0:T(8,128)} all-to-all(f32[8,8,48,128]{3,2,1,0:T(8,128)S(1)} %broadcast_in_dim.4), channel_id=1, replica_groups=mesh['z2'=4,'z1'=2,'x'=4,'y'=8,'c'=2] {'z1','x'}, dimensions={0} | all-to-all | bytes 3145728 | tf_op jit(solution)/shard_map/all_to_all | solution.py:208
  51.0 9.0 %shard_map.52 = f32[768,128]{1,0:T(8,128)} custom-call(s32[1]{0:T(128)} %bitcast.1.core_ref, bf16[2,768,1536]{2,1,0:T(8,128)(2,1)} %get-tuple-element.13.mine_ref, bf16[2,768,1536]{2,1,0:T(8,128)(2,1)} %get-tuple-element.14.theirs_ref, f32[8,8,48,128]{3,2,1,0:T(8,128)} %all_to_all.30.x_ref), custom_call_target="tpu_custom_call" | custom-call | flops 2415919104 | bytes 9437184 | tf_op jit(solution)/shard_map/pallas_call | solution.py:115
  60.0 6.8 %all-to-all-start.2 = ((f32[8,96,128]{2,1,0:T(8,128)}), f32[8,96,128]{2,1,0:T(8,128)S(1)}, u32[]{:S(2)}, u32[]{:S(2)}) async-start(f32[8,96,128]{2,1,0:T(8,128)} %bitcast.21), calls=%async_computation.2 | async-start | bytes 786432 | tf_op jit(solution)/shard_map/all_to_all | solution.py:212
  66.9 0.8 slice_bitcast_fusion
  67.6 10.7 %all-to-all-done.2 = f32[8,96,128]{2,1,0:T(8,128)S(1)} async-done(((f32[8,96,128]{2,1,0:T(8,128)}), f32[8,96,128]{2,1,0:T(8,128)S(1)}, u32[]{:S(2)}, u32[]{:S(2)}) %all-to-all-start.2) | async-done | bytes 393248 | tf_op jit(solution)/shard_map/all_to_all | solution.py:212
  78.5 13.9 %all_to_all.31.y_ref = f32[8,96,128]{2,1,0:T(8,128)} all-to-all(f32[8,96,128]{2,1,0:T(8,128)S(1)} %broadcast_in_dim.5), channel_id=1, replica_groups=mesh['z2'=4,'z1'=2,'x'=4,'y'=8,'c'=2] {'y'}, dimensions={0} | all-to-all | bytes 786432 | tf_op jit(solution)/shard_map/all_to_all | solution.py:215
  92.3 10.9 %shard_map.53 = f32[8,8,48,128]{3,2,1,0:T(8,128)} custom-call(s32[1]{0:T(128)} %bitcast.1.core_ref, bf16[2,768,1536]{2,1,0:T(8,128)(2,1)} %get-tuple-element.13.mine_ref, bf16[2,768,1536]{2,1,0:T(8,128)(2,1)} %get-tuple-element.14.theirs_ref, f32[8,96,128]{2,1,0:T(8,128)} %all_to_all.31.y_ref), custom_call_target="tpu_custom_call" | custom-call | flops 2415919104 | bytes 9437184 | tf_op jit(solution)/shard_map/pallas_call | solution.py:170
  103.2 4.9 %all-to-all-start.4 = ((f32[8,8,48,128]{3,2,1,0:T(8,128)}), f32[8,8,48,128]{3,2,1,0:T(8,128)S(1)}, u32[]{:S(2)}, u32[]{:S(2)}) async-start(f32[8,8,48,128]{3,2,1,0:T(8,128)} %shard_map.53), calls=%async_computation.4 | async-start | bytes 3145728 | tf_op jit(solution)/shard_map/all_to_all | solution.py:224
  108.1 15.8 %all-to-all-done.4 = f32[8,8,48,128]{3,2,1,0:T(8,128)S(1)} async-done(((f32[8,8,48,128]{3,2,1,0:T(8,128)}), f32[8,8,48,128]{3,2,1,0:T(8,128)S(1)}, u32[]{:S(2)}, u32[]{:S(2)}) %all-to-all-start.4) | async-done | bytes 1572896 | tf_op jit(solution)/shard_map/all_to_all | solution.py:224
  124.0 0.8 reduce_sum.31
  124.7 13.6 %all-to-all-start.5 = ((f32[8,48,128]{2,1,0:T(8,128)}), f32[8,48,128]{2,1,0:T(8,128)S(1)}, u32[]{:S(2)}, u32[]{:S(2)}) async-start(f32[8,48,128]{2,1,0:T(8,128)} %reduce_sum.31), calls=%async_computation.5 | async-start | bytes 393216 | tf_op jit(solution)/shard_map/all_to_all | solution.py:225
  138.4 1.9 %collective-permute-start.1 = (f32[48,128]{1,0:T(8,128)S(1)}, f32[48,128]{1,0:T(8,128)S(1)}, u32[]{:S(2)}, u32[]{:S(2)}) collective-permute-start(f32[48,128]{1,0:T(8,128)S(1)} %get-tuple-element.17), channel_id=1, source_target_pairs={{0,1},{1,0},{2,3},{3,2},{4,5},{5,4},{6,7},{7,6},{8,9},{9,8},{10,11... | collective-permute-start | bytes 73736 | tf_op jit(solution)/shard_map/ppermute | solution.py:220
  140.3 0.7 slice.11
  141.1 0.5 collective-permute-done.1
  141.5 0.6 maximum_select_fusion
  142.1 6.2 %all-to-all-done.5 = f32[8,48,128]{2,1,0:T(8,128)S(1)} async-done(((f32[8,48,128]{2,1,0:T(8,128)}), f32[8,48,128]{2,1,0:T(8,128)S(1)}, u32[]{:S(2)}, u32[]{:S(2)}) %all-to-all-start.5) | async-done | bytes 196640 | tf_op jit(solution)/shard_map/all_to_all | solution.py:225
  148.4 0.6 bitcast_subtract_fusion
  (9 shorter events, 0.1 us)
Async XLA Ops:
  0.6 16.7 %collective-permute-start = (f32[768,1536]{1,0:T(8,128)}, f32[768,1536]{1,0:T(8,128)}, u32[]{:S(2)}, u32[]{:S(2)}) collective-permute-start(f32[768,1536]{1,0:T(8,128)} %mine_ref.1), channel_id=1, source_target_pairs={{0,1},{1,0},{2,3},{3,2},{4,5},{5,4},{6,7},{7,6},{8,9},{9,8},{10,11... | collective-permute-start | bytes 14155784 | tf_op jit(solution)/shard_map/ppermute | solution.py:199
  10.9 15.8 %all-to-all-start = ((f32[8,48,128]{2,1,0:T(8,128)}), f32[8,48,128]{2,1,0:T(8,128)S(1)}, u32[]{:S(2)}, u32[]{:S(2)}) async-start(f32[8,48,128]{2,1,0:T(8,128)} %bitcast.22), calls=%async_computation | async-start | bytes 393216 | tf_op jit(solution)/shard_map/all_to_all | solution.py:204
  60.0 18.3 %all-to-all-start.2 = ((f32[8,96,128]{2,1,0:T(8,128)}), f32[8,96,128]{2,1,0:T(8,128)S(1)}, u32[]{:S(2)}, u32[]{:S(2)}) async-start(f32[8,96,128]{2,1,0:T(8,128)} %bitcast.21), calls=%async_computation.2 | async-start | bytes 786432 | tf_op jit(solution)/shard_map/all_to_all | solution.py:212
  103.2 45.1 %copy-start = (f32[48,256]{1,0:T(8,128)S(1)}, f32[48,256]{1,0:T(8,128)}, u32[]{:S(2)}) copy-start(f32[48,256]{1,0:T(8,128)} %search_ref.1) | copy-start | bytes 147460
  103.2 20.8 %all-to-all-start.4 = ((f32[8,8,48,128]{3,2,1,0:T(8,128)}), f32[8,8,48,128]{3,2,1,0:T(8,128)S(1)}, u32[]{:S(2)}, u32[]{:S(2)}) async-start(f32[8,8,48,128]{3,2,1,0:T(8,128)} %shard_map.53), calls=%async_computation.4 | async-start | bytes 3145728 | tf_op jit(solution)/shard_map/all_to_all | solution.py:224
  124.7 23.6 %all-to-all-start.5 = ((f32[8,48,128]{2,1,0:T(8,128)}), f32[8,48,128]{2,1,0:T(8,128)S(1)}, u32[]{:S(2)}, u32[]{:S(2)}) async-start(f32[8,48,128]{2,1,0:T(8,128)} %reduce_sum.31), calls=%async_computation.5 | async-start | bytes 393216 | tf_op jit(solution)/shard_map/all_to_all | solution.py:225
  138.4 3.1 %collective-permute-start.1 = (f32[48,128]{1,0:T(8,128)S(1)}, f32[48,128]{1,0:T(8,128)S(1)}, u32[]{:S(2)}, u32[]{:S(2)}) collective-permute-start(f32[48,128]{1,0:T(8,128)S(1)} %get-tuple-element.17), channel_id=1, source_target_pairs={{0,1},{1,0},{2,3},{3,2},{4,5},{5,4},{6,7},{7,6},{8,9},{9,8},{10,11... | collective-permute-start | bytes 73736 | tf_op jit(solution)/shard_map/ppermute | solution.py:220

commit v4 on v2

v4 whole, which is shorter than its diff:
```python
import jax
import jax.numpy as jnp
from jax import lax
from jax.experimental import pallas as pl
from jax.experimental.pallas import tpu as pltpu
from jax.sharding import Mesh, PartitionSpec as P

BF, F32 = jnp.bfloat16, jnp.float32
SMEM = pl.BlockSpec(memory_space=pltpu.SMEM)
PARAMS = pltpu.CompilerParams(vmem_limit_bytes=60 * 1024 * 1024)


def split(v):
    hi = v.astype(BF)
    return hi, (v - hi.astype(F32)).astype(BF)


def deal_kernel(search_ref, out_ref):
    part = out_ref.shape[-1]
    for zi in range(out_ref.shape[0]):
        for ci in range(out_ref.shape[1]):
            out_ref[zi, ci] = search_ref[:, ci * part : (ci + 1) * part]


def split_kernel(place_ref, bounds_ref, mine_ref, theirs_ref, out_ref, scalars_ref):
    rows, cols = mine_ref.shape
    core = place_ref[0]
    center = (bounds_ref[2] + bounds_ref[1]) / 2.0
    row = lax.broadcasted_iota(jnp.int32, (rows, cols), 0)
    col = lax.broadcasted_iota(jnp.int32, (rows, cols), 1)
    apart = col - row
    for block, tile_ref in ((core, mine_ref), (1 - core, theirs_ref)):
        offset = place_ref[1] + pl.program_id(0) * rows - block * cols
        hi, lo = split(tile_ref[...] - jnp.where(apart == offset, center, 0.0))
        out_ref[block, 0] = hi
        out_ref[block, 1] = lo

    @pl.when(pl.program_id(0) == 0)
    def _():
        lower, low_end, high_end = (jnp.full((1, scalars_ref.shape[1]), bounds_ref[i], F32) for i in range(3))
        center = (high_end + low_end) / 2.0
        half = (high_end - low_end) / 2.0
        sigma_one = half / (lower - center)
        sigma_two = 1.0 / (2.0 / sigma_one - sigma_one)
        scalars_ref[0:1] = sigma_one / half
        scalars_ref[1:2] = 2.0 * sigma_two / half
        scalars_ref[2:3] = sigma_two * sigma_one


def split_tiles(place, bounds, mine, theirs, width, step=128):
    rows, cols = mine.shape
    tile = pl.BlockSpec((step, cols), lambda i: (i, 0))
    out = pl.BlockSpec((2, 2, step, cols), lambda i: (0, 0, i, 0))
    return pl.pallas_call(
        split_kernel,
        grid=(rows // step,),
        in_specs=[SMEM, SMEM, tile, tile],
        out_specs=(out, pl.BlockSpec((8, width), lambda i: (0, 0))),
        out_shape=(
            jax.ShapeDtypeStruct((2, 2, rows, cols), BF),
            jax.ShapeDtypeStruct((8, width), F32),
        ),
        compiler_params=PARAMS,
        cost_estimate=pl.CostEstimate(flops=16 * rows * cols, bytes_accessed=16 * rows * cols, transcendentals=0),
    )(place, bounds, mine, theirs)


def rows_kernel(h_ref, x_ref, out_ref, wide):
    xs, zc, piece, part = x_ref.shape

    @pl.when(pl.program_id(0) == 0)
    def _():
        for zi in range(zc // 2):
            for block in range(2):
                for xi in range(xs):
                    hi, lo = split(x_ref[xi, zi * 2 + block])
                    at = pl.ds((zi * xs + xi) * piece, piece)
                    wide[block, at, :part] = hi
                    wide[block, at, part:] = lo

    step, cols = h_ref.shape[2:]
    acc = jnp.dot(h_ref[0].reshape(2 * step, cols), wide[0], preferred_element_type=F32)
    acc += jnp.dot(h_ref[1].reshape(2 * step, cols), wide[1], preferred_element_type=F32)
    acc = acc[:, :part] + acc[:, part:]
    out_ref[...] = acc[:step] + acc[step:]


def rows_product(h, x, step=256):
    _, _, rows, cols = h.shape
    xs, zc, piece, part = x.shape
    return pl.pallas_call(
        rows_kernel,
        grid=(rows // step,),
        in_specs=[
            pl.BlockSpec((2, 2, step, cols), lambda i: (0, 0, i, 0)),
            pl.BlockSpec(x.shape, lambda i: (0, 0, 0, 0)),
        ],
        out_specs=pl.BlockSpec((step, part), lambda i: (i, 0)),
        out_shape=jax.ShapeDtypeStruct((rows, part), F32),
        scratch_shapes=[pltpu.VMEM((2, cols, 2 * part), BF)],
        compiler_params=PARAMS,
        cost_estimate=pl.CostEstimate(
            flops=16 * rows * cols * part, bytes_accessed=8 * rows * cols, transcendentals=0
        ),
    )(h, x)


def cols_kernel(h_ref, y_ref, out_ref, tall):
    xs, zs, _, piece, part = out_ref.shape

    @pl.when((pl.program_id(0) == 0) & (pl.program_id(1) == 0))
    def _():
        share = y_ref.shape[1]
        flat = y_ref[...].reshape(y_ref.shape[0] * share, part).T
        hi, lo = split(flat)
        tall[:part] = hi
        tall[part:] = lo

    acc = jnp.dot(tall[...], h_ref[0, 0], preferred_element_type=F32)
    acc += jnp.dot(tall[...], h_ref[0, 1], preferred_element_type=F32)
    out = (acc[:part] + acc[part:]).T
    for zi in range(zs):
        for xi in range(xs):
            at = (zi * xs + xi) * piece
            out_ref[xi, zi, 0] = out[at : at + piece]


def cols_product(h, y, xs, zs, steps=2):
    _, _, rows, cols = h.shape
    part = y.shape[-1]
    piece = cols // (xs * zs)
    return pl.pallas_call(
        cols_kernel,
        grid=(2, steps),
        in_specs=[
            pl.BlockSpec((1, 2, rows, cols // steps), lambda b, j: (b, 0, 0, j)),
            pl.BlockSpec(y.shape, lambda b, j: (0, 0, 0)),
        ],
        out_specs=pl.BlockSpec((xs, zs // steps, 1, piece, part), lambda b, j: (0, j, b, 0, 0)),
        out_shape=jax.ShapeDtypeStruct((xs, zs, 2, piece, part), F32),
        scratch_shapes=[pltpu.VMEM((2 * part, rows), BF)],
        compiler_params=PARAMS,
        cost_estimate=pl.CostEstimate(
            flops=16 * rows * cols * part, bytes_accessed=8 * rows * cols, transcendentals=0
        ),
    )(h, y)


def body(hamiltonian, search_block, filter_bounds):
    z2s, z1s, xs, ys, cs = (lax.axis_size(a) for a in ("z2", "z1", "x", "y", "c"))
    z2, z1, x, y, c = (lax.axis_index(a) for a in ("z2", "z1", "x", "y", "c"))
    rows_tile, cols_tile = hamiltonian.shape
    piece, width = search_block.shape
    part = width // cs
    outer = z1s * xs
    swap = [(i, cs - 1 - i) for i in range(cs)]

    first_row = ((z2 * z1s + z1) * xs + x) * rows_tile
    first_col = y * cs * cols_tile
    other = lax.ppermute(hamiltonian, "c", swap)
    place = jnp.stack([c, first_row - first_col]).astype(jnp.int32)
    tiles, scalars = split_tiles(place, filter_bounds, hamiltonian, other, width)

    sent = pl.pallas_call(deal_kernel, out_shape=jax.ShapeDtypeStruct((z2s, cs, piece, part), F32))(search_block)
    got = lax.all_to_all(sent.reshape(z2s * cs, piece, part), ("z2", "c"), 0, 0, tiled=True)
    got, tiles, scalars = lax.optimization_barrier((got, tiles, scalars))
    scale_one, scale_two, damp = scalars[0, :part], scalars[1, :part], scalars[2]
    sent = jnp.broadcast_to(got[None], (outer,) + got.shape)
    got = lax.all_to_all(sent, ("z1", "x"), 0, 0, tiled=True)

    partial_rows = rows_product(tiles, got)
    share = rows_tile // ys
    terms = lax.all_to_all(partial_rows.reshape(ys, share, part), "y", 0, 0, tiled=True)
    first = scale_one * terms.sum(0)
    sent = jnp.broadcast_to(first[None], terms.shape)
    first_rows = lax.all_to_all(sent, "y", 0, 0, tiled=True)

    first_pair = first.reshape(cs, piece, part)
    keep = lax.dynamic_index_in_dim(first_pair, c, 0, keepdims=False)
    give = lax.dynamic_index_in_dim(first_pair, cs - 1 - c, 0, keepdims=False)
    came = lax.ppermute(give, "c", swap)
    first_out = jnp.where(c == 0, jnp.concatenate([keep, came], 1), jnp.concatenate([came, keep], 1))

    sent = cols_product(tiles, first_rows, outer, z2s).reshape(outer, z2s * cs, piece, part)
    summed = lax.all_to_all(sent, ("z1", "x"), 0, 0, tiled=True).sum(0)
    summed = lax.all_to_all(summed, ("z2", "c"), 0, 0, tiled=True)
    summed = scale_two * summed.reshape(z2s, cs, piece, part).sum(0)
    second_out = summed.transpose(1, 0, 2).reshape(piece, width) - damp * search_block
    return (first_out, second_out)


def solution(mesh):
    fine = Mesh(mesh.devices.reshape(4, 2, 4, 8, 2), ("z2", "z1", "x", "y", "c"))
    row, col = ("z2", "z1", "x"), ("y", "c")
    return jax.shard_map(
        body,
        mesh=fine,
        in_specs=(P(row, col), P(col + row, None), P()),
        out_specs=(P(row + col, None), P(col + row, None)),
        check_vma=False,
    )
```

time: 156 us -> 145 us (0.929)
  blocking collectives: 57.7 us -> 37.8 us
  local copies, waits for them, and re-layouts: 16.1 us -> 1.63 us
  starting transfers between devices: 27.8 us -> 39.2 us
  Pallas kernels: 15.3 us -> 25.6 us
  waiting for transfers between devices: 32.3 us -> 36 us
  between operations: 4.06 us -> 0.71 us
    all_to_all x2 -> x1, blocking collectives: 41 us -> 24.1 us  [body(): got = lax.all_to_all(sent, ('z1', 'x'), 0, 0, tiled=True)]
    unnamed x12 -> x2, local copies, waits for them, and re-layouts: 13.3 us -> 0.01 us
    all_to_all x2 -> x3, starting transfers between devices: 10 us -> 21.6 us  [the longest x1 8.39 us: body(): summed = lax.all_to_all(summed, ('z2', 'c'), 0, 0, tiled=True)]
    all_to_all x2 -> x3, waiting for transfers between devices: 18.3 us -> 23.7 us  [the longest x1 17.5 us: body(): summed = lax.all_to_all(sent, ('z1', 'x'), 0, 0, tiled=True).sum(0)]
    pallas_call x1 -> x2, Pallas kernels: 5.81 us -> 11.1 us  [the longest x1 9.61 us: split_tiles(): pl.pallas_call(split_kernel, grid=(rows // step,), in_specs=[SMEM, SMEM,...]
    all_to_all x1, blocking collectives: 16.7 us -> 13.7 us  [body(): first_rows = lax.all_to_all(sent, 'y', 0, 0, tiled=True)]
    pallas_call x1, Pallas kernels: 4.46 us -> 7.32 us  [cols_product(): pl.pallas_call(cols_kernel, grid=(2, steps), in_specs=[pl.BlockSpec((1, 2...]
    pallas_call x1, Pallas kernels: 5.07 us -> 7.17 us  [rows_product(): pl.pallas_call(rows_kernel, grid=(rows // step,), in_specs=[pl.BlockSpec(...]
  transfers between devices with their start and end apart: 5 -> 6, of which waited for: 4 -> 5; matrix products, arithmetic and copies ran while one was open for 2% -> 2% of each run, Pallas kernels for 4% -> 8%
where the time goes in v4:
time: 145 us; the launch traced here: 144 us
  starting transfers between devices  39.2 us (27%)
  blocking collectives  37.8 us (26%)
  waiting for transfers between devices  36 us (25%)
  Pallas kernels  25.6 us (18%)
  other arithmetic  2.7 us (2%)
  local copies, waits for them, and re-layouts  1.63 us (1%)
    all_to_all x1, blocking collectives, body(): got = lax.all_to_all(sent, ('z1', 'x'), 0, 0, tiled=True)  24.1 us
    all_to_all x1, waiting for transfers between devices, body(): summed = lax.all_to_all(sent, ('z1', 'x'), 0, 0, tiled=True).sum(0)  17.5 us
    all_to_all x1, blocking collectives, body(): first_rows = lax.all_to_all(sent, 'y', 0, 0, tiled=True)  13.7 us
    all_to_all x1, waiting for transfers between devices, body(): lax.all_to_all(partial_rows.reshape(ys, share, part), 'y', 0, 0, tiled=True)  11.1 us
    pallas_call x1, Pallas kernels, split_tiles(): pl.pallas_call(split_kernel, grid=(rows // step,), in_specs=[SMEM, SMEM,...  9.61 us
    ppermute x1, starting transfers between devices, body(): other = lax.ppermute(hamiltonian, 'c', swap)  8.79 us
    all_to_all x1, starting transfers between devices, body(): summed = lax.all_to_all(summed, ('z2', 'c'), 0, 0, tiled=True)  8.39 us
    all_to_all x1, starting transfers between devices, body(): summed = lax.all_to_all(sent, ('z1', 'x'), 0, 0, tiled=True).sum(0)  8.21 us
  transfers between devices with their start and end apart: 6, of which 5 were waited for; matrix products, arithmetic and copies ran while one was open for 2% of the time, Pallas kernels for 8%

profile of v4, /device:TPU:1, one launch (start us, length us, event | category | flops | bytes accessed | tf_op | source)
XLA Modules:
  0.0 143.6 jit_solution(10249010304923290605)
XLA Ops:
  0.6 8.8 %collective-permute-start = (f32[768,1536]{1,0:T(8,128)}, f32[768,1536]{1,0:T(8,128)}, u32[]{:S(2)}, u32[]{:S(2)}) collective-permute-start(f32[768,1536]{1,0:T(8,128)} %mine_ref.1), channel_id=1, source_target_pairs={{0,1},{1,0},{2,3},{3,2},{4,5},{5,4},{6,7},{7,6},{8,9},{9,8},{10,11... | collective-permute-start | bytes 14155784 | tf_op jit(solution)/shard_map/ppermute | solution.py:160
  9.4 1.5 %shard_map.50 = f32[4,2,48,128]{3,2,1,0:T(8,128)} custom-call(f32[48,256]{1,0:T(8,128)} %search_ref.1), custom_call_target="tpu_custom_call" | custom-call | tf_op jit(solution)/shard_map/pallas_call | solution.py:164
  10.9 5.0 %all-to-all-start = ((f32[8,48,128]{2,1,0:T(8,128)}), f32[8,48,128]{2,1,0:T(8,128)S(1)}, u32[]{:S(2)}, u32[]{:S(2)}) async-start(f32[8,48,128]{2,1,0:T(8,128)} %bitcast.24), calls=%async_computation | async-start | bytes 393216 | tf_op jit(solution)/shard_map/all_to_all | solution.py:165
  15.9 0.6 pad_add_fusion.place_ref
  16.6 0.7 collective-permute-done.theirs_ref
  17.3 9.6 %shard_map.51 = (bf16[2,2,768,1536]{3,2,1,0:T(8,128)(2,1)}, f32[8,256]{1,0:T(8,128)}) custom-call(s32[2]{0:T(128)} %pad_add_fusion.place_ref, f32[3]{0:T(128)} %bounds_ref.1, f32[768,1536]{1,0:T(8,128)} %mine_ref.1, f32[768,1536]{1,0:T(8,128)} %collective-permute-done.theirs_ref), custom_call_target="tpu_custom_call" | custom-call | flops 18874368 | bytes 18874368 | tf_op jit(solution)/shard_map/pallas_call | solution.py:54
  26.9 0.1 broadcast_in_dim.4
  27.0 24.1 %all_to_all.30.x_ref = f32[8,8,48,128]{3,2,1,0:T(8,128)} all-to-all(f32[8,8,48,128]{3,2,1,0:T(8,128)S(1)} %broadcast_in_dim.4), channel_id=1, replica_groups=mesh['z2'=4,'z1'=2,'x'=4,'y'=8,'c'=2] {'z1','x'}, dimensions={0} | all-to-all | bytes 3145728 | tf_op jit(solution)/shard_map/all_to_all | solution.py:169
  51.2 7.2 %shard_map.52 = f32[768,128]{1,0:T(8,128)} custom-call(bf16[2,2,768,1536]{3,2,1,0:T(8,128)(2,1)} %get-tuple-element.10.h_ref, f32[8,8,48,128]{3,2,1,0:T(8,128)} %all_to_all.30.x_ref), custom_call_target="tpu_custom_call" | custom-call | flops 2415919104 | bytes 9437184 | tf_op jit(solution)/shard_map/pallas_call | solution.py:91
  58.3 6.8 %all-to-all-start.2 = ((f32[8,96,128]{2,1,0:T(8,128)}), f32[8,96,128]{2,1,0:T(8,128)S(1)}, u32[]{:S(2)}, u32[]{:S(2)}) async-start(f32[8,96,128]{2,1,0:T(8,128)} %bitcast.23), calls=%async_computation.2 | async-start | bytes 786432 | tf_op jit(solution)/shard_map/all_to_all | solution.py:173
  65.2 0.8 slice_bitcast_fusion
  65.9 11.1 %all-to-all-done.2 = f32[8,96,128]{2,1,0:T(8,128)S(1)} async-done(((f32[8,96,128]{2,1,0:T(8,128)}), f32[8,96,128]{2,1,0:T(8,128)S(1)}, u32[]{:S(2)}, u32[]{:S(2)}) %all-to-all-start.2) | async-done | bytes 393248 | tf_op jit(solution)/shard_map/all_to_all | solution.py:173
  77.1 13.7 %all_to_all.31.y_ref = f32[8,96,128]{2,1,0:T(8,128)} all-to-all(f32[8,96,128]{2,1,0:T(8,128)S(1)} %broadcast_in_dim.5), channel_id=1, replica_groups=mesh['z2'=4,'z1'=2,'x'=4,'y'=8,'c'=2] {'y'}, dimensions={0} | all-to-all | bytes 786432 | tf_op jit(solution)/shard_map/all_to_all | solution.py:176
  90.8 7.3 %shard_map.53 = f32[8,4,2,48,128]{4,3,2,1,0:T(8,128)} custom-call(bf16[2,2,768,1536]{3,2,1,0:T(8,128)(2,1)} %get-tuple-element.10.h_ref, f32[8,96,128]{2,1,0:T(8,128)} %all_to_all.31.y_ref), custom_call_target="tpu_custom_call" | custom-call | flops 2415919104 | bytes 9437184 | tf_op jit(solution)/shard_map/pallas_call | solution.py:132
  98.1 8.2 %all-to-all-start.4 = ((f32[8,8,48,128]{3,2,1,0:T(8,128)}), f32[8,8,48,128]{3,2,1,0:T(8,128)S(1)}, u32[]{:S(2)}, u32[]{:S(2)}) async-start(f32[8,8,48,128]{3,2,1,0:T(8,128)} %bitcast.22), calls=%async_computation.4 | async-start | bytes 3145728 | tf_op jit(solution)/shard_map/all_to_all | solution.py:185
  106.3 17.5 %all-to-all-done.4 = f32[8,8,48,128]{3,2,1,0:T(8,128)S(1)} async-done(((f32[8,8,48,128]{3,2,1,0:T(8,128)}), f32[8,8,48,128]{3,2,1,0:T(8,128)S(1)}, u32[]{:S(2)}, u32[]{:S(2)}) %all-to-all-start.4) | async-done | bytes 1572896 | tf_op jit(solution)/shard_map/all_to_all | solution.py:185
  123.8 0.8 reduce_sum.31
  124.6 8.4 %all-to-all-start.5 = ((f32[8,48,128]{2,1,0:T(8,128)}), f32[8,48,128]{2,1,0:T(8,128)S(1)}, u32[]{:S(2)}, u32[]{:S(2)}) async-start(f32[8,48,128]{2,1,0:T(8,128)} %reduce_sum.31), calls=%async_computation.5 | async-start | bytes 393216 | tf_op jit(solution)/shard_map/all_to_all | solution.py:186
  133.0 1.9 %collective-permute-start.1 = (f32[48,128]{1,0:T(8,128)S(1)}, f32[48,128]{1,0:T(8,128)S(1)}, u32[]{:S(2)}, u32[]{:S(2)}) collective-permute-start(f32[48,128]{1,0:T(8,128)S(1)} %get-tuple-element.13), channel_id=1, source_target_pairs={{0,1},{1,0},{2,3},{3,2},{4,5},{5,4},{6,7},{7,6},{8,9},{9,8},{10,11... | collective-permute-start | bytes 73736 | tf_op jit(solution)/shard_map/ppermute | solution.py:181
  134.9 0.7 slice.11
  135.6 0.5 collective-permute-done.1
  136.1 0.6 maximum_select_fusion
  136.7 6.2 %all-to-all-done.5 = f32[8,48,128]{2,1,0:T(8,128)S(1)} async-done(((f32[8,48,128]{2,1,0:T(8,128)}), f32[8,48,128]{2,1,0:T(8,128)S(1)}, u32[]{:S(2)}, u32[]{:S(2)}) %all-to-all-start.5) | async-done | bytes 196640 | tf_op jit(solution)/shard_map/all_to_all | solution.py:186
  142.9 0.6 bitcast_subtract_fusion
  (9 shorter events, 0.1 us)
Async XLA Ops:
  0.6 16.7 %collective-permute-start = (f32[768,1536]{1,0:T(8,128)}, f32[768,1536]{1,0:T(8,128)}, u32[]{:S(2)}, u32[]{:S(2)}) collective-permute-start(f32[768,1536]{1,0:T(8,128)} %mine_ref.1), channel_id=1, source_target_pairs={{0,1},{1,0},{2,3},{3,2},{4,5},{5,4},{6,7},{7,6},{8,9},{9,8},{10,11... | collective-permute-start | bytes 14155784 | tf_op jit(solution)/shard_map/ppermute | solution.py:160
  10.9 16.0 %all-to-all-start = ((f32[8,48,128]{2,1,0:T(8,128)}), f32[8,48,128]{2,1,0:T(8,128)S(1)}, u32[]{:S(2)}, u32[]{:S(2)}) async-start(f32[8,48,128]{2,1,0:T(8,128)} %bitcast.24), calls=%async_computation | async-start | bytes 393216 | tf_op jit(solution)/shard_map/all_to_all | solution.py:165
  58.3 18.7 %all-to-all-start.2 = ((f32[8,96,128]{2,1,0:T(8,128)}), f32[8,96,128]{2,1,0:T(8,128)S(1)}, u32[]{:S(2)}, u32[]{:S(2)}) async-start(f32[8,96,128]{2,1,0:T(8,128)} %bitcast.23), calls=%async_computation.2 | async-start | bytes 786432 | tf_op jit(solution)/shard_map/all_to_all | solution.py:173
  98.1 25.7 %all-to-all-start.4 = ((f32[8,8,48,128]{3,2,1,0:T(8,128)}), f32[8,8,48,128]{3,2,1,0:T(8,128)S(1)}, u32[]{:S(2)}, u32[]{:S(2)}) async-start(f32[8,8,48,128]{3,2,1,0:T(8,128)} %bitcast.22), calls=%async_computation.4 | async-start | bytes 3145728 | tf_op jit(solution)/shard_map/all_to_all | solution.py:185
  106.3 36.6 %copy-start = (f32[48,256]{1,0:T(8,128)S(1)}, f32[48,256]{1,0:T(8,128)}, u32[]{:S(2)}) copy-start(f32[48,256]{1,0:T(8,128)} %search_ref.1) | copy-start | bytes 147460
  124.6 18.4 %all-to-all-start.5 = ((f32[8,48,128]{2,1,0:T(8,128)}), f32[8,48,128]{2,1,0:T(8,128)S(1)}, u32[]{:S(2)}, u32[]{:S(2)}) async-start(f32[8,48,128]{2,1,0:T(8,128)} %reduce_sum.31), calls=%async_computation.5 | async-start | bytes 393216 | tf_op jit(solution)/shard_map/all_to_all | solution.py:186
  133.0 3.1 %collective-permute-start.1 = (f32[48,128]{1,0:T(8,128)S(1)}, f32[48,128]{1,0:T(8,128)S(1)}, u32[]{:S(2)}, u32[]{:S(2)}) collective-permute-start(f32[48,128]{1,0:T(8,128)S(1)} %get-tuple-element.13), channel_id=1, source_target_pairs={{0,1},{1,0},{2,3},{3,2},{4,5},{5,4},{6,7},{7,6},{8,9},{9,8},{10,11... | collective-permute-start | bytes 73736 | tf_op jit(solution)/shard_map/ppermute | solution.py:181

commit v5 on v4

--- a/solution.py
+++ b/solution.py
@@ -7,7 +7,7 @@
 
 BF, F32 = jnp.bfloat16, jnp.float32
 SMEM = pl.BlockSpec(memory_space=pltpu.SMEM)
-PARAMS = pltpu.CompilerParams(vmem_limit_bytes=60 * 1024 * 1024)
+PARAMS = pltpu.CompilerParams(vmem_limit_bytes=56 * 1024 * 1024)
 
 
 def split(v):
@@ -47,7 +47,7 @@
         scalars_ref[2:3] = sigma_two * sigma_one
 
 
-def split_tiles(place, bounds, mine, theirs, width, step=128):
+def split_tiles(place, bounds, mine, theirs, width, step=256):
     rows, cols = mine.shape
     tile = pl.BlockSpec((step, cols), lambda i: (i, 0))
     out = pl.BlockSpec((2, 2, step, cols), lambda i: (0, 0, i, 0))
@@ -85,7 +85,7 @@
     out_ref[...] = acc[:step] + acc[step:]
 
 
-def rows_product(h, x, step=256):
+def rows_product(h, x, step=384):
     _, _, rows, cols = h.shape
     xs, zc, piece, part = x.shape
     return pl.pallas_call(
@@ -125,7 +125,7 @@
             out_ref[xi, zi, 0] = out[at : at + piece]
 
 
-def cols_product(h, y, xs, zs, steps=2):
+def cols_product(h, y, xs, zs, steps=1):
     _, _, rows, cols = h.shape
     part = y.shape[-1]
     piece = cols // (xs * zs)

time: 145 us -> 143 us (0.986)
  starting transfers between devices: 39.2 us -> 36.7 us
  waiting for transfers between devices: 36 us -> 38.5 us
    all_to_all x1, starting transfers between devices: 8.39 us -> 4.73 us  [body(): summed = lax.all_to_all(summed, ('z2', 'c'), 0, 0, tiled=True)]
    all_to_all x1, waiting for transfers between devices: 17.5 us -> 20 us  [body(): summed = lax.all_to_all(sent, ('z1', 'x'), 0, 0, tiled=True).sum(0)]
where the time goes in v5:
time: 143 us; the launch traced here: 142 us
  waiting for transfers between devices  38.5 us (27%)
  blocking collectives  37.8 us (26%)
  starting transfers between devices  36.7 us (26%)
  Pallas kernels  24.3 us (17%)
  other arithmetic  2.7 us (2%)
  local copies, waits for them, and re-layouts  1.63 us (1%)
    all_to_all x1, blocking collectives, body(): got = lax.all_to_all(sent, ('z1', 'x'), 0, 0, tiled=True)  24.1 us
    all_to_all x1, waiting for transfers between devices, body(): summed = lax.all_to_all(sent, ('z1', 'x'), 0, 0, tiled=True).sum(0)  20 us
    all_to_all x1, blocking collectives, body(): first_rows = lax.all_to_all(sent, 'y', 0, 0, tiled=True)  13.7 us
    all_to_all x1, waiting for transfers between devices, body(): lax.all_to_all(partial_rows.reshape(ys, share, part), 'y', 0, 0, tiled=True)  11.2 us
    pallas_call x1, Pallas kernels, split_tiles(): pl.pallas_call(split_kernel, grid=(rows // step,), in_specs=[SMEM, SMEM,...  9.73 us
    all_to_all x1, starting transfers between devices, body(): summed = lax.all_to_all(sent, ('z1', 'x'), 0, 0, tiled=True).sum(0)  9.4 us
    ppermute x1, starting transfers between devices, body(): other = lax.ppermute(hamiltonian, 'c', swap)  8.79 us
    all_to_all x1, starting transfers between devices, body(): lax.all_to_all(partial_rows.reshape(ys, share, part), 'y', 0, 0, tiled=True)  6.82 us
  transfers between devices with their start and end apart: 6, of which 5 were waited for; matrix products, arithmetic and copies ran while one was open for 2% of the time, Pallas kernels for 8%

profile of v5, /device:TPU:1, one launch (start us, length us, event | category | flops | bytes accessed | tf_op | source)
XLA Modules:
  0.0 142.4 jit_solution(3220014171839229437)
XLA Ops:
  0.6 8.8 %collective-permute-start = (f32[768,1536]{1,0:T(8,128)}, f32[768,1536]{1,0:T(8,128)}, u32[]{:S(2)}, u32[]{:S(2)}) collective-permute-start(f32[768,1536]{1,0:T(8,128)} %mine_ref.1), channel_id=1, source_target_pairs={{0,1},{1,0},{2,3},{3,2},{4,5},{5,4},{6,7},{7,6},{8,9},{9,8},{10,11... | collective-permute-start | bytes 14155784 | tf_op jit(solution)/shard_map/ppermute | solution.py:160
  9.4 1.5 %shard_map.50 = f32[4,2,48,128]{3,2,1,0:T(8,128)} custom-call(f32[48,256]{1,0:T(8,128)} %search_ref.1), custom_call_target="tpu_custom_call" | custom-call | tf_op jit(solution)/shard_map/pallas_call | solution.py:164
  10.9 5.0 %all-to-all-start = ((f32[8,48,128]{2,1,0:T(8,128)}), f32[8,48,128]{2,1,0:T(8,128)S(1)}, u32[]{:S(2)}, u32[]{:S(2)}) async-start(f32[8,48,128]{2,1,0:T(8,128)} %bitcast.24), calls=%async_computation | async-start | bytes 393216 | tf_op jit(solution)/shard_map/all_to_all | solution.py:165
  15.9 0.6 pad_add_fusion.place_ref
  16.6 0.7 collective-permute-done.theirs_ref
  17.3 9.7 %shard_map.51 = (bf16[2,2,768,1536]{3,2,1,0:T(8,128)(2,1)}, f32[8,256]{1,0:T(8,128)}) custom-call(s32[2]{0:T(128)} %pad_add_fusion.place_ref, f32[3]{0:T(128)} %bounds_ref.1, f32[768,1536]{1,0:T(8,128)} %mine_ref.1, f32[768,1536]{1,0:T(8,128)} %collective-permute-done.theirs_ref), custom_call_target="tpu_custom_call" | custom-call | flops 18874368 | bytes 18874368 | tf_op jit(solution)/shard_map/pallas_call | solution.py:54
  27.0 0.1 broadcast_in_dim.4
  27.1 24.1 %all_to_all.30.x_ref = f32[8,8,48,128]{3,2,1,0:T(8,128)} all-to-all(f32[8,8,48,128]{3,2,1,0:T(8,128)S(1)} %broadcast_in_dim.4), channel_id=1, replica_groups=mesh['z2'=4,'z1'=2,'x'=4,'y'=8,'c'=2] {'z1','x'}, dimensions={0} | all-to-all | bytes 3145728 | tf_op jit(solution)/shard_map/all_to_all | solution.py:169
  51.3 6.6 %shard_map.52 = f32[768,128]{1,0:T(8,128)} custom-call(bf16[2,2,768,1536]{3,2,1,0:T(8,128)(2,1)} %get-tuple-element.10.h_ref, f32[8,8,48,128]{3,2,1,0:T(8,128)} %all_to_all.30.x_ref), custom_call_target="tpu_custom_call" | custom-call | flops 2415919104 | bytes 9437184 | tf_op jit(solution)/shard_map/pallas_call | solution.py:91
  57.8 6.8 %all-to-all-start.2 = ((f32[8,96,128]{2,1,0:T(8,128)}), f32[8,96,128]{2,1,0:T(8,128)S(1)}, u32[]{:S(2)}, u32[]{:S(2)}) async-start(f32[8,96,128]{2,1,0:T(8,128)} %bitcast.23), calls=%async_computation.2 | async-start | bytes 786432 | tf_op jit(solution)/shard_map/all_to_all | solution.py:173
  64.7 0.8 slice_bitcast_fusion
  65.4 11.2 %all-to-all-done.2 = f32[8,96,128]{2,1,0:T(8,128)S(1)} async-done(((f32[8,96,128]{2,1,0:T(8,128)}), f32[8,96,128]{2,1,0:T(8,128)S(1)}, u32[]{:S(2)}, u32[]{:S(2)}) %all-to-all-start.2) | async-done | bytes 393248 | tf_op jit(solution)/shard_map/all_to_all | solution.py:173
  76.7 13.7 %all_to_all.31.y_ref = f32[8,96,128]{2,1,0:T(8,128)} all-to-all(f32[8,96,128]{2,1,0:T(8,128)S(1)} %broadcast_in_dim.5), channel_id=1, replica_groups=mesh['z2'=4,'z1'=2,'x'=4,'y'=8,'c'=2] {'y'}, dimensions={0} | all-to-all | bytes 786432 | tf_op jit(solution)/shard_map/all_to_all | solution.py:176
  90.3 6.5 %shard_map.53 = f32[8,4,2,48,128]{4,3,2,1,0:T(8,128)} custom-call(bf16[2,2,768,1536]{3,2,1,0:T(8,128)(2,1)} %get-tuple-element.10.h_ref, f32[8,96,128]{2,1,0:T(8,128)} %all_to_all.31.y_ref), custom_call_target="tpu_custom_call" | custom-call | flops 2415919104 | bytes 9437184 | tf_op jit(solution)/shard_map/pallas_call | solution.py:132
  96.9 9.4 %all-to-all-start.4 = ((f32[8,8,48,128]{3,2,1,0:T(8,128)}), f32[8,8,48,128]{3,2,1,0:T(8,128)S(1)}, u32[]{:S(2)}, u32[]{:S(2)}) async-start(f32[8,8,48,128]{3,2,1,0:T(8,128)} %bitcast.22), calls=%async_computation.4 | async-start | bytes 3145728 | tf_op jit(solution)/shard_map/all_to_all | solution.py:185
  106.3 20.0 %all-to-all-done.4 = f32[8,8,48,128]{3,2,1,0:T(8,128)S(1)} async-done(((f32[8,8,48,128]{3,2,1,0:T(8,128)}), f32[8,8,48,128]{3,2,1,0:T(8,128)S(1)}, u32[]{:S(2)}, u32[]{:S(2)}) %all-to-all-start.4) | async-done | bytes 1572896 | tf_op jit(solution)/shard_map/all_to_all | solution.py:185
  126.3 0.8 reduce_sum.31
  127.0 4.7 %all-to-all-start.5 = ((f32[8,48,128]{2,1,0:T(8,128)}), f32[8,48,128]{2,1,0:T(8,128)S(1)}, u32[]{:S(2)}, u32[]{:S(2)}) async-start(f32[8,48,128]{2,1,0:T(8,128)} %reduce_sum.31), calls=%async_computation.5 | async-start | bytes 393216 | tf_op jit(solution)/shard_map/all_to_all | solution.py:186
  131.8 2.0 %collective-permute-start.1 = (f32[48,128]{1,0:T(8,128)S(1)}, f32[48,128]{1,0:T(8,128)S(1)}, u32[]{:S(2)}, u32[]{:S(2)}) collective-permute-start(f32[48,128]{1,0:T(8,128)S(1)} %get-tuple-element.13), channel_id=1, source_target_pairs={{0,1},{1,0},{2,3},{3,2},{4,5},{5,4},{6,7},{7,6},{8,9},{9,8},{10,11... | collective-permute-start | bytes 73736 | tf_op jit(solution)/shard_map/ppermute | solution.py:181
  133.8 0.7 slice.11
  134.5 0.4 collective-permute-done.1
  134.9 0.6 maximum_select_fusion
  135.5 6.2 %all-to-all-done.5 = f32[8,48,128]{2,1,0:T(8,128)S(1)} async-done(((f32[8,48,128]{2,1,0:T(8,128)}), f32[8,48,128]{2,1,0:T(8,128)S(1)}, u32[]{:S(2)}, u32[]{:S(2)}) %all-to-all-start.5) | async-done | bytes 196640 | tf_op jit(solution)/shard_map/all_to_all | solution.py:186
  141.7 0.6 bitcast_subtract_fusion
  (9 shorter events, 0.1 us)
Async XLA Ops:
  0.6 16.7 %collective-permute-start = (f32[768,1536]{1,0:T(8,128)}, f32[768,1536]{1,0:T(8,128)}, u32[]{:S(2)}, u32[]{:S(2)}) collective-permute-start(f32[768,1536]{1,0:T(8,128)} %mine_ref.1), channel_id=1, source_target_pairs={{0,1},{1,0},{2,3},{3,2},{4,5},{5,4},{6,7},{7,6},{8,9},{9,8},{10,11... | collective-permute-start | bytes 14155784 | tf_op jit(solution)/shard_map/ppermute | solution.py:160
  10.9 16.1 %all-to-all-start = ((f32[8,48,128]{2,1,0:T(8,128)}), f32[8,48,128]{2,1,0:T(8,128)S(1)}, u32[]{:S(2)}, u32[]{:S(2)}) async-start(f32[8,48,128]{2,1,0:T(8,128)} %bitcast.24), calls=%async_computation | async-start | bytes 393216 | tf_op jit(solution)/shard_map/all_to_all | solution.py:165
  57.8 18.7 %all-to-all-start.2 = ((f32[8,96,128]{2,1,0:T(8,128)}), f32[8,96,128]{2,1,0:T(8,128)S(1)}, u32[]{:S(2)}, u32[]{:S(2)}) async-start(f32[8,96,128]{2,1,0:T(8,128)} %bitcast.23), calls=%async_computation.2 | async-start | bytes 786432 | tf_op jit(solution)/shard_map/all_to_all | solution.py:173
  96.9 29.4 %all-to-all-start.4 = ((f32[8,8,48,128]{3,2,1,0:T(8,128)}), f32[8,8,48,128]{3,2,1,0:T(8,128)S(1)}, u32[]{:S(2)}, u32[]{:S(2)}) async-start(f32[8,8,48,128]{3,2,1,0:T(8,128)} %bitcast.22), calls=%async_computation.4 | async-start | bytes 3145728 | tf_op jit(solution)/shard_map/all_to_all | solution.py:185
  106.3 35.5 %copy-start = (f32[48,256]{1,0:T(8,128)S(1)}, f32[48,256]{1,0:T(8,128)}, u32[]{:S(2)}) copy-start(f32[48,256]{1,0:T(8,128)} %search_ref.1) | copy-start | bytes 147460
  127.0 14.7 %all-to-all-start.5 = ((f32[8,48,128]{2,1,0:T(8,128)}), f32[8,48,128]{2,1,0:T(8,128)S(1)}, u32[]{:S(2)}, u32[]{:S(2)}) async-start(f32[8,48,128]{2,1,0:T(8,128)} %reduce_sum.31), calls=%async_computation.5 | async-start | bytes 393216 | tf_op jit(solution)/shard_map/all_to_all | solution.py:186
  131.8 3.1 %collective-permute-start.1 = (f32[48,128]{1,0:T(8,128)S(1)}, f32[48,128]{1,0:T(8,128)S(1)}, u32[]{:S(2)}, u32[]{:S(2)}) collective-permute-start(f32[48,128]{1,0:T(8,128)S(1)} %get-tuple-element.13), channel_id=1, source_target_pairs={{0,1},{1,0},{2,3},{3,2},{4,5},{5,4},{6,7},{7,6},{8,9},{9,8},{10,11... | collective-permute-start | bytes 73736 | tf_op jit(solution)/shard_map/ppermute | solution.py:181

commit v6 on v5

--- a/solution.py
+++ b/solution.py
@@ -47,7 +47,7 @@
         scalars_ref[2:3] = sigma_two * sigma_one
 
 
-def split_tiles(place, bounds, mine, theirs, width, step=256):
+def split_tiles(place, bounds, mine, theirs, width, step=384):
     rows, cols = mine.shape
     tile = pl.BlockSpec((step, cols), lambda i: (i, 0))
     out = pl.BlockSpec((2, 2, step, cols), lambda i: (0, 0, i, 0))

time: 143 us -> 141 us (0.986)
  waiting for transfers between devices: 38.5 us -> 33.7 us
  starting transfers between devices: 36.7 us -> 41.4 us
  Pallas kernels: 24.3 us -> 22.2 us
    all_to_all x1, starting transfers between devices: 4.73 us -> 14.6 us  [body(): summed = lax.all_to_all(summed, ('z2', 'c'), 0, 0, tiled=True)]
    all_to_all x1, starting transfers between devices: 9.4 us -> 4.2 us  [body(): summed = lax.all_to_all(sent, ('z1', 'x'), 0, 0, tiled=True).sum(0)]
    all_to_all x1, waiting for transfers between devices: 20 us -> 15.3 us  [body(): summed = lax.all_to_all(sent, ('z1', 'x'), 0, 0, tiled=True).sum(0)]
    pallas_call x1, Pallas kernels: 9.73 us -> 7.62 us  [split_tiles(): pl.pallas_call(split_kernel, grid=(rows // step,), in_specs=[SMEM, SMEM,...]
  transfers between devices with their start and end apart: 6 -> 6, of which waited for: 5 -> 6; matrix products, arithmetic and copies ran while one was open for 2% -> 2% of each run, Pallas kernels for 8% -> 6%
where the time goes in v6:
time: 141 us; the launch traced here: 140 us
  starting transfers between devices  41.4 us (29%)
  blocking collectives  38 us (27%)
  waiting for transfers between devices  33.7 us (24%)
  Pallas kernels  22.2 us (16%)
  other arithmetic  2.7 us (2%)
  local copies, waits for them, and re-layouts  1.63 us (1%)
    all_to_all x1, blocking collectives, body(): got = lax.all_to_all(sent, ('z1', 'x'), 0, 0, tiled=True)  23.7 us
    all_to_all x1, waiting for transfers between devices, body(): summed = lax.all_to_all(sent, ('z1', 'x'), 0, 0, tiled=True).sum(0)  15.3 us
    all_to_all x1, starting transfers between devices, body(): summed = lax.all_to_all(summed, ('z2', 'c'), 0, 0, tiled=True)  14.6 us
    all_to_all x1, blocking collectives, body(): first_rows = lax.all_to_all(sent, 'y', 0, 0, tiled=True)  14.3 us
    all_to_all x1, waiting for transfers between devices, body(): lax.all_to_all(partial_rows.reshape(ys, share, part), 'y', 0, 0, tiled=True)  9.98 us
    ppermute x1, starting transfers between devices, body(): other = lax.ppermute(hamiltonian, 'c', swap)  8.79 us
    pallas_call x1, Pallas kernels, split_tiles(): pl.pallas_call(split_kernel, grid=(rows // step,), in_specs=[SMEM, SMEM,...  7.62 us
    all_to_all x1, starting transfers between devices, body(): lax.all_to_all(partial_rows.reshape(ys, share, part), 'y', 0, 0, tiled=True)  6.82 us
  transfers between devices with their start and end apart: 6, of which 6 were waited for; matrix products, arithmetic and copies ran while one was open for 2% of the time, Pallas kernels for 6%

profile of v6, /device:TPU:1, one launch (start us, length us, event | category | flops | bytes accessed | tf_op | source)
XLA Modules:
  0.0 140.3 jit_solution(11627494964764712340)
XLA Ops:
  0.6 8.8 %collective-permute-start = (f32[768,1536]{1,0:T(8,128)}, f32[768,1536]{1,0:T(8,128)}, u32[]{:S(2)}, u32[]{:S(2)}) collective-permute-start(f32[768,1536]{1,0:T(8,128)} %mine_ref.1), channel_id=1, source_target_pairs={{0,1},{1,0},{2,3},{3,2},{4,5},{5,4},{6,7},{7,6},{8,9},{9,8},{10,11... | collective-permute-start | bytes 14155784 | tf_op jit(solution)/shard_map/ppermute | solution.py:160
  9.4 1.5 %shard_map.50 = f32[4,2,48,128]{3,2,1,0:T(8,128)} custom-call(f32[48,256]{1,0:T(8,128)} %search_ref.1), custom_call_target="tpu_custom_call" | custom-call | tf_op jit(solution)/shard_map/pallas_call | solution.py:164
  10.9 5.0 %all-to-all-start = ((f32[8,48,128]{2,1,0:T(8,128)}), f32[8,48,128]{2,1,0:T(8,128)S(1)}, u32[]{:S(2)}, u32[]{:S(2)}) async-start(f32[8,48,128]{2,1,0:T(8,128)} %bitcast.24), calls=%async_computation | async-start | bytes 393216 | tf_op jit(solution)/shard_map/all_to_all | solution.py:165
  15.9 0.6 pad_add_fusion.place_ref
  16.6 0.7 collective-permute-done.theirs_ref
  17.3 7.6 %shard_map.51 = (bf16[2,2,768,1536]{3,2,1,0:T(8,128)(2,1)}, f32[8,256]{1,0:T(8,128)}) custom-call(s32[2]{0:T(128)} %pad_add_fusion.place_ref, f32[3]{0:T(128)} %bounds_ref.1, f32[768,1536]{1,0:T(8,128)} %mine_ref.1, f32[768,1536]{1,0:T(8,128)} %collective-permute-done.theirs_ref), custom_call_target="tpu_custom_call" | custom-call | flops 18874368 | bytes 18874368 | tf_op jit(solution)/shard_map/pallas_call | solution.py:54
  24.9 1.0 all-to-all-done
  26.0 23.7 %all_to_all.30.x_ref = f32[8,8,48,128]{3,2,1,0:T(8,128)} all-to-all(f32[8,8,48,128]{3,2,1,0:T(8,128)S(1)} %broadcast_in_dim.4), channel_id=1, replica_groups=mesh['z2'=4,'z1'=2,'x'=4,'y'=8,'c'=2] {'z1','x'}, dimensions={0} | all-to-all | bytes 3145728 | tf_op jit(solution)/shard_map/all_to_all | solution.py:169
  49.8 6.6 %shard_map.52 = f32[768,128]{1,0:T(8,128)} custom-call(bf16[2,2,768,1536]{3,2,1,0:T(8,128)(2,1)} %get-tuple-element.10.h_ref, f32[8,8,48,128]{3,2,1,0:T(8,128)} %all_to_all.30.x_ref), custom_call_target="tpu_custom_call" | custom-call | flops 2415919104 | bytes 9437184 | tf_op jit(solution)/shard_map/pallas_call | solution.py:91
  56.3 6.8 %all-to-all-start.2 = ((f32[8,96,128]{2,1,0:T(8,128)}), f32[8,96,128]{2,1,0:T(8,128)S(1)}, u32[]{:S(2)}, u32[]{:S(2)}) async-start(f32[8,96,128]{2,1,0:T(8,128)} %bitcast.23), calls=%async_computation.2 | async-start | bytes 786432 | tf_op jit(solution)/shard_map/all_to_all | solution.py:173
  63.2 0.8 slice_bitcast_fusion
  63.9 10.0 %all-to-all-done.2 = f32[8,96,128]{2,1,0:T(8,128)S(1)} async-done(((f32[8,96,128]{2,1,0:T(8,128)}), f32[8,96,128]{2,1,0:T(8,128)S(1)}, u32[]{:S(2)}, u32[]{:S(2)}) %all-to-all-start.2) | async-done | bytes 393248 | tf_op jit(solution)/shard_map/all_to_all | solution.py:173
  74.0 14.3 %all_to_all.31.y_ref = f32[8,96,128]{2,1,0:T(8,128)} all-to-all(f32[8,96,128]{2,1,0:T(8,128)S(1)} %broadcast_in_dim.5), channel_id=1, replica_groups=mesh['z2'=4,'z1'=2,'x'=4,'y'=8,'c'=2] {'y'}, dimensions={0} | all-to-all | bytes 786432 | tf_op jit(solution)/shard_map/all_to_all | solution.py:176
  88.2 6.5 %shard_map.53 = f32[8,4,2,48,128]{4,3,2,1,0:T(8,128)} custom-call(bf16[2,2,768,1536]{3,2,1,0:T(8,128)(2,1)} %get-tuple-element.10.h_ref, f32[8,96,128]{2,1,0:T(8,128)} %all_to_all.31.y_ref), custom_call_target="tpu_custom_call" | custom-call | flops 2415919104 | bytes 9437184 | tf_op jit(solution)/shard_map/pallas_call | solution.py:132
  94.8 4.2 %all-to-all-start.4 = ((f32[8,8,48,128]{3,2,1,0:T(8,128)}), f32[8,8,48,128]{3,2,1,0:T(8,128)S(1)}, u32[]{:S(2)}, u32[]{:S(2)}) async-start(f32[8,8,48,128]{3,2,1,0:T(8,128)} %bitcast.22), calls=%async_computation.4 | async-start | bytes 3145728 | tf_op jit(solution)/shard_map/all_to_all | solution.py:185
  99.0 15.3 %all-to-all-done.4 = f32[8,8,48,128]{3,2,1,0:T(8,128)S(1)} async-done(((f32[8,8,48,128]{3,2,1,0:T(8,128)}), f32[8,8,48,128]{3,2,1,0:T(8,128)S(1)}, u32[]{:S(2)}, u32[]{:S(2)}) %all-to-all-start.4) | async-done | bytes 1572896 | tf_op jit(solution)/shard_map/all_to_all | solution.py:185
  114.3 0.8 reduce_sum.31
  115.1 14.6 %all-to-all-start.5 = ((f32[8,48,128]{2,1,0:T(8,128)}), f32[8,48,128]{2,1,0:T(8,128)S(1)}, u32[]{:S(2)}, u32[]{:S(2)}) async-start(f32[8,48,128]{2,1,0:T(8,128)} %reduce_sum.31), calls=%async_computation.5 | async-start | bytes 393216 | tf_op jit(solution)/shard_map/all_to_all | solution.py:186
  129.7 1.9 %collective-permute-start.1 = (f32[48,128]{1,0:T(8,128)S(1)}, f32[48,128]{1,0:T(8,128)S(1)}, u32[]{:S(2)}, u32[]{:S(2)}) collective-permute-start(f32[48,128]{1,0:T(8,128)S(1)} %get-tuple-element.13), channel_id=1, source_target_pairs={{0,1},{1,0},{2,3},{3,2},{4,5},{5,4},{6,7},{7,6},{8,9},{9,8},{10,11... | collective-permute-start | bytes 73736 | tf_op jit(solution)/shard_map/ppermute | solution.py:181
  131.6 0.7 slice.11
  132.3 0.5 collective-permute-done.1
  132.8 0.6 maximum_select_fusion
  133.4 6.2 %all-to-all-done.5 = f32[8,48,128]{2,1,0:T(8,128)S(1)} async-done(((f32[8,48,128]{2,1,0:T(8,128)}), f32[8,48,128]{2,1,0:T(8,128)S(1)}, u32[]{:S(2)}, u32[]{:S(2)}) %all-to-all-start.5) | async-done | bytes 196640 | tf_op jit(solution)/shard_map/all_to_all | solution.py:186
  139.6 0.6 bitcast_subtract_fusion
  (9 shorter events, 0.2 us)
Async XLA Ops:
  0.6 16.7 %collective-permute-start = (f32[768,1536]{1,0:T(8,128)}, f32[768,1536]{1,0:T(8,128)}, u32[]{:S(2)}, u32[]{:S(2)}) collective-permute-start(f32[768,1536]{1,0:T(8,128)} %mine_ref.1), channel_id=1, source_target_pairs={{0,1},{1,0},{2,3},{3,2},{4,5},{5,4},{6,7},{7,6},{8,9},{9,8},{10,11... | collective-permute-start | bytes 14155784 | tf_op jit(solution)/shard_map/ppermute | solution.py:160
  10.9 15.0 %all-to-all-start = ((f32[8,48,128]{2,1,0:T(8,128)}), f32[8,48,128]{2,1,0:T(8,128)S(1)}, u32[]{:S(2)}, u32[]{:S(2)}) async-start(f32[8,48,128]{2,1,0:T(8,128)} %bitcast.24), calls=%async_computation | async-start | bytes 393216 | tf_op jit(solution)/shard_map/all_to_all | solution.py:165
  56.3 17.6 %all-to-all-start.2 = ((f32[8,96,128]{2,1,0:T(8,128)}), f32[8,96,128]{2,1,0:T(8,128)S(1)}, u32[]{:S(2)}, u32[]{:S(2)}) async-start(f32[8,96,128]{2,1,0:T(8,128)} %bitcast.23), calls=%async_computation.2 | async-start | bytes 786432 | tf_op jit(solution)/shard_map/all_to_all | solution.py:173
  94.8 19.5 %all-to-all-start.4 = ((f32[8,8,48,128]{3,2,1,0:T(8,128)}), f32[8,8,48,128]{3,2,1,0:T(8,128)S(1)}, u32[]{:S(2)}, u32[]{:S(2)}) async-start(f32[8,8,48,128]{3,2,1,0:T(8,128)} %bitcast.22), calls=%async_computation.4 | async-start | bytes 3145728 | tf_op jit(solution)/shard_map/all_to_all | solution.py:185
  99.0 40.6 %copy-start = (f32[48,256]{1,0:T(8,128)S(1)}, f32[48,256]{1,0:T(8,128)}, u32[]{:S(2)}) copy-start(f32[48,256]{1,0:T(8,128)} %search_ref.1) | copy-start | bytes 147460
  115.1 24.6 %all-to-all-start.5 = ((f32[8,48,128]{2,1,0:T(8,128)}), f32[8,48,128]{2,1,0:T(8,128)S(1)}, u32[]{:S(2)}, u32[]{:S(2)}) async-start(f32[8,48,128]{2,1,0:T(8,128)} %reduce_sum.31), calls=%async_computation.5 | async-start | bytes 393216 | tf_op jit(solution)/shard_map/all_to_all | solution.py:186
  129.7 3.1 %collective-permute-start.1 = (f32[48,128]{1,0:T(8,128)S(1)}, f32[48,128]{1,0:T(8,128)S(1)}, u32[]{:S(2)}, u32[]{:S(2)}) collective-permute-start(f32[48,128]{1,0:T(8,128)S(1)} %get-tuple-element.13), channel_id=1, source_target_pairs={{0,1},{1,0},{2,3},{3,2},{4,5},{5,4},{6,7},{7,6},{8,9},{9,8},{10,11... | collective-permute-start | bytes 73736 | tf_op jit(solution)/shard_map/ppermute | solution.py:181

commit v7 on v6

--- a/solution.py
+++ b/solution.py
@@ -157,11 +157,12 @@
 
     first_row = ((z2 * z1s + z1) * xs + x) * rows_tile
     first_col = y * cs * cols_tile
+    sent = pl.pallas_call(deal_kernel, out_shape=jax.ShapeDtypeStruct((z2s, cs, piece, part), F32))(search_block)
+    hamiltonian, sent = lax.optimization_barrier((hamiltonian, sent))
     other = lax.ppermute(hamiltonian, "c", swap)
     place = jnp.stack([c, first_row - first_col]).astype(jnp.int32)
     tiles, scalars = split_tiles(place, filter_bounds, hamiltonian, other, width)
 
-    sent = pl.pallas_call(deal_kernel, out_shape=jax.ShapeDtypeStruct((z2s, cs, piece, part), F32))(search_block)
     got = lax.all_to_all(sent.reshape(z2s * cs, piece, part), ("z2", "c"), 0, 0, tiled=True)
     got, tiles, scalars = lax.optimization_barrier((got, tiles, scalars))
     scale_one, scale_two, damp = scalars[0, :part], scalars[1, :part], scalars[2]

time: 141 us -> 141 us (level)
    ppermute x1, waiting for transfers between devices: 0.7 us -> 2.17 us  [body(): other = lax.ppermute(hamiltonian, 'c', swap)]
  transfers between devices with their start and end apart: 6 -> 6, of which waited for: 6 -> 5; matrix products, arithmetic and copies ran while one was open for 2% -> 2% of each run, Pallas kernels for 6% -> 5%
where the time goes in v7:
time: 141 us; the launch traced here: 140 us
  starting transfers between devices  41.6 us (30%)
  blocking collectives  37.5 us (27%)
  waiting for transfers between devices  34.1 us (24%)
  Pallas kernels  22.2 us (16%)
  other arithmetic  2.7 us (2%)
  local copies, waits for them, and re-layouts  1.63 us (1%)
    all_to_all x1, blocking collectives, body(): got = lax.all_to_all(sent, ('z1', 'x'), 0, 0, tiled=True)  23.3 us
    all_to_all x1, waiting for transfers between devices, body(): summed = lax.all_to_all(sent, ('z1', 'x'), 0, 0, tiled=True).sum(0)  15.3 us
    all_to_all x1, starting transfers between devices, body(): summed = lax.all_to_all(summed, ('z2', 'c'), 0, 0, tiled=True)  14.8 us
    all_to_all x1, blocking collectives, body(): first_rows = lax.all_to_all(sent, 'y', 0, 0, tiled=True)  14.3 us
    all_to_all x1, waiting for transfers between devices, body(): lax.all_to_all(partial_rows.reshape(ys, share, part), 'y', 0, 0, tiled=True)  9.98 us
    ppermute x1, starting transfers between devices, body(): other = lax.ppermute(hamiltonian, 'c', swap)  8.78 us
    pallas_call x1, Pallas kernels, split_tiles(): pl.pallas_call(split_kernel, grid=(rows // step,), in_specs=[SMEM, SMEM,...  7.62 us
    all_to_all x1, starting transfers between devices, body(): lax.all_to_all(partial_rows.reshape(ys, share, part), 'y', 0, 0, tiled=True)  6.82 us
  transfers between devices with their start and end apart: 6, of which 5 were waited for; matrix products, arithmetic and copies ran while one was open for 2% of the time, Pallas kernels for 5%

profile of v7, /device:TPU:1, one launch (start us, length us, event | category | flops | bytes accessed | tf_op | source)
XLA Modules:
  0.0 140.5 jit_solution(13575438368818967470)
XLA Ops:
  0.6 1.5 %shard_map.50 = f32[4,2,48,128]{3,2,1,0:T(8,128)} custom-call(f32[48,256]{1,0:T(8,128)} %search_ref.1), custom_call_target="tpu_custom_call" | custom-call | tf_op jit(solution)/shard_map/pallas_call | solution.py:160
  2.1 8.8 %collective-permute-start = (f32[768,1536]{1,0:T(8,128)}, f32[768,1536]{1,0:T(8,128)}, u32[]{:S(2)}, u32[]{:S(2)}) collective-permute-start(f32[768,1536]{1,0:T(8,128)} %mine_ref), channel_id=1, source_target_pairs={{0,1},{1,0},{2,3},{3,2},{4,5},{5,4},{6,7},{7,6},{8,9},{9,8},{10,11... | collective-permute-start | bytes 14155784 | tf_op jit(solution)/shard_map/ppermute | solution.py:162
  10.9 5.1 %all-to-all-start = ((f32[8,48,128]{2,1,0:T(8,128)}), f32[8,48,128]{2,1,0:T(8,128)S(1)}, u32[]{:S(2)}, u32[]{:S(2)}) async-start(f32[8,48,128]{2,1,0:T(8,128)} %bitcast.24), calls=%async_computation | async-start | bytes 393216 | tf_op jit(solution)/shard_map/all_to_all | solution.py:166
  15.9 0.6 pad_add_fusion.place_ref
  16.6 2.2 %collective-permute-done.theirs_ref = f32[768,1536]{1,0:T(8,128)} collective-permute-done((f32[768,1536]{1,0:T(8,128)}, f32[768,1536]{1,0:T(8,128)}, u32[]{:S(2)}, u32[]{:S(2)}) %collective-permute-start) | collective-permute-done | bytes 4718624 | tf_op jit(solution)/shard_map/ppermute | solution.py:162
  18.7 7.6 %shard_map.51 = (bf16[2,2,768,1536]{3,2,1,0:T(8,128)(2,1)}, f32[8,256]{1,0:T(8,128)}) custom-call(s32[2]{0:T(128)} %pad_add_fusion.place_ref, f32[3]{0:T(128)} %bounds_ref.1, f32[768,1536]{1,0:T(8,128)} %mine_ref, f32[768,1536]{1,0:T(8,128)} %collective-permute-done.theirs_ref), custom_call_target="tpu_custom_call" | custom-call | flops 18874368 | bytes 18874368 | tf_op jit(solution)/shard_map/pallas_call | solution.py:54
  26.4 0.1 broadcast_in_dim.4
  26.5 23.3 %all_to_all.30.x_ref = f32[8,8,48,128]{3,2,1,0:T(8,128)} all-to-all(f32[8,8,48,128]{3,2,1,0:T(8,128)S(1)} %broadcast_in_dim.4), channel_id=1, replica_groups=mesh['z2'=4,'z1'=2,'x'=4,'y'=8,'c'=2] {'z1','x'}, dimensions={0} | all-to-all | bytes 3145728 | tf_op jit(solution)/shard_map/all_to_all | solution.py:170
  49.8 6.6 %shard_map.52 = f32[768,128]{1,0:T(8,128)} custom-call(bf16[2,2,768,1536]{3,2,1,0:T(8,128)(2,1)} %get-tuple-element.14.h_ref, f32[8,8,48,128]{3,2,1,0:T(8,128)} %all_to_all.30.x_ref), custom_call_target="tpu_custom_call" | custom-call | flops 2415919104 | bytes 9437184 | tf_op jit(solution)/shard_map/pallas_call | solution.py:91
  56.3 6.8 %all-to-all-start.2 = ((f32[8,96,128]{2,1,0:T(8,128)}), f32[8,96,128]{2,1,0:T(8,128)S(1)}, u32[]{:S(2)}, u32[]{:S(2)}) async-start(f32[8,96,128]{2,1,0:T(8,128)} %bitcast.23), calls=%async_computation.2 | async-start | bytes 786432 | tf_op jit(solution)/shard_map/all_to_all | solution.py:174
  63.2 0.8 slice_bitcast_fusion
  63.9 10.0 %all-to-all-done.2 = f32[8,96,128]{2,1,0:T(8,128)S(1)} async-done(((f32[8,96,128]{2,1,0:T(8,128)}), f32[8,96,128]{2,1,0:T(8,128)S(1)}, u32[]{:S(2)}, u32[]{:S(2)}) %all-to-all-start.2) | async-done | bytes 393248 | tf_op jit(solution)/shard_map/all_to_all | solution.py:174
  74.0 14.3 %all_to_all.31.y_ref = f32[8,96,128]{2,1,0:T(8,128)} all-to-all(f32[8,96,128]{2,1,0:T(8,128)S(1)} %broadcast_in_dim.5), channel_id=1, replica_groups=mesh['z2'=4,'z1'=2,'x'=4,'y'=8,'c'=2] {'y'}, dimensions={0} | all-to-all | bytes 786432 | tf_op jit(solution)/shard_map/all_to_all | solution.py:177
  88.2 6.5 %shard_map.53 = f32[8,4,2,48,128]{4,3,2,1,0:T(8,128)} custom-call(bf16[2,2,768,1536]{3,2,1,0:T(8,128)(2,1)} %get-tuple-element.14.h_ref, f32[8,96,128]{2,1,0:T(8,128)} %all_to_all.31.y_ref), custom_call_target="tpu_custom_call" | custom-call | flops 2415919104 | bytes 9437184 | tf_op jit(solution)/shard_map/pallas_call | solution.py:132
  94.8 4.2 %all-to-all-start.4 = ((f32[8,8,48,128]{3,2,1,0:T(8,128)}), f32[8,8,48,128]{3,2,1,0:T(8,128)S(1)}, u32[]{:S(2)}, u32[]{:S(2)}) async-start(f32[8,8,48,128]{3,2,1,0:T(8,128)} %bitcast.22), calls=%async_computation.4 | async-start | bytes 3145728 | tf_op jit(solution)/shard_map/all_to_all | solution.py:186
  99.0 15.3 %all-to-all-done.4 = f32[8,8,48,128]{3,2,1,0:T(8,128)S(1)} async-done(((f32[8,8,48,128]{3,2,1,0:T(8,128)}), f32[8,8,48,128]{3,2,1,0:T(8,128)S(1)}, u32[]{:S(2)}, u32[]{:S(2)}) %all-to-all-start.4) | async-done | bytes 1572896 | tf_op jit(solution)/shard_map/all_to_all | solution.py:186
  114.3 0.8 reduce_sum.31
  115.1 14.8 %all-to-all-start.5 = ((f32[8,48,128]{2,1,0:T(8,128)}), f32[8,48,128]{2,1,0:T(8,128)S(1)}, u32[]{:S(2)}, u32[]{:S(2)}) async-start(f32[8,48,128]{2,1,0:T(8,128)} %reduce_sum.31), calls=%async_computation.5 | async-start | bytes 393216 | tf_op jit(solution)/shard_map/all_to_all | solution.py:187
  129.9 1.9 %collective-permute-start.1 = (f32[48,128]{1,0:T(8,128)S(1)}, f32[48,128]{1,0:T(8,128)S(1)}, u32[]{:S(2)}, u32[]{:S(2)}) collective-permute-start(f32[48,128]{1,0:T(8,128)S(1)} %get-tuple-element.17), channel_id=1, source_target_pairs={{0,1},{1,0},{2,3},{3,2},{4,5},{5,4},{6,7},{7,6},{8,9},{9,8},{10,11... | collective-permute-start | bytes 73736 | tf_op jit(solution)/shard_map/ppermute | solution.py:182
  131.8 0.7 slice.11
  132.5 0.5 collective-permute-done.1
  133.0 0.6 maximum_select_fusion
  133.6 6.2 %all-to-all-done.5 = f32[8,48,128]{2,1,0:T(8,128)S(1)} async-done(((f32[8,48,128]{2,1,0:T(8,128)}), f32[8,48,128]{2,1,0:T(8,128)S(1)}, u32[]{:S(2)}, u32[]{:S(2)}) %all-to-all-start.5) | async-done | bytes 196640 | tf_op jit(solution)/shard_map/all_to_all | solution.py:187
  139.9 0.6 bitcast_subtract_fusion
  (9 shorter events, 0.1 us)
Async XLA Ops:
  2.1 16.6 %collective-permute-start = (f32[768,1536]{1,0:T(8,128)}, f32[768,1536]{1,0:T(8,128)}, u32[]{:S(2)}, u32[]{:S(2)}) collective-permute-start(f32[768,1536]{1,0:T(8,128)} %mine_ref), channel_id=1, source_target_pairs={{0,1},{1,0},{2,3},{3,2},{4,5},{5,4},{6,7},{7,6},{8,9},{9,8},{10,11... | collective-permute-start | bytes 14155784 | tf_op jit(solution)/shard_map/ppermute | solution.py:162
  10.9 15.5 %all-to-all-start = ((f32[8,48,128]{2,1,0:T(8,128)}), f32[8,48,128]{2,1,0:T(8,128)S(1)}, u32[]{:S(2)}, u32[]{:S(2)}) async-start(f32[8,48,128]{2,1,0:T(8,128)} %bitcast.24), calls=%async_computation | async-start | bytes 393216 | tf_op jit(solution)/shard_map/all_to_all | solution.py:166
  56.3 17.6 %all-to-all-start.2 = ((f32[8,96,128]{2,1,0:T(8,128)}), f32[8,96,128]{2,1,0:T(8,128)S(1)}, u32[]{:S(2)}, u32[]{:S(2)}) async-start(f32[8,96,128]{2,1,0:T(8,128)} %bitcast.23), calls=%async_computation.2 | async-start | bytes 786432 | tf_op jit(solution)/shard_map/all_to_all | solution.py:174
  94.8 19.5 %all-to-all-start.4 = ((f32[8,8,48,128]{3,2,1,0:T(8,128)}), f32[8,8,48,128]{3,2,1,0:T(8,128)S(1)}, u32[]{:S(2)}, u32[]{:S(2)}) async-start(f32[8,8,48,128]{3,2,1,0:T(8,128)} %bitcast.22), calls=%async_computation.4 | async-start | bytes 3145728 | tf_op jit(solution)/shard_map/all_to_all | solution.py:186
  99.0 40.9 %copy-start = (f32[48,256]{1,0:T(8,128)S(1)}, f32[48,256]{1,0:T(8,128)}, u32[]{:S(2)}) copy-start(f32[48,256]{1,0:T(8,128)} %search_ref.1) | copy-start | bytes 147460
  115.1 24.8 %all-to-all-start.5 = ((f32[8,48,128]{2,1,0:T(8,128)}), f32[8,48,128]{2,1,0:T(8,128)S(1)}, u32[]{:S(2)}, u32[]{:S(2)}) async-start(f32[8,48,128]{2,1,0:T(8,128)} %reduce_sum.31), calls=%async_computation.5 | async-start | bytes 393216 | tf_op jit(solution)/shard_map/all_to_all | solution.py:187
  129.9 3.1 %collective-permute-start.1 = (f32[48,128]{1,0:T(8,128)S(1)}, f32[48,128]{1,0:T(8,128)S(1)}, u32[]{:S(2)}, u32[]{:S(2)}) collective-permute-start(f32[48,128]{1,0:T(8,128)S(1)} %get-tuple-element.17), channel_id=1, source_target_pairs={{0,1},{1,0},{2,3},{3,2},{4,5},{5,4},{6,7},{7,6},{8,9},{9,8},{10,11... | collective-permute-start | bytes 73736 | tf_op jit(solution)/shard_map/ppermute | solution.py:182
